TPU v7x, 32 devices: a whole 2x2x4 slice. The times are simulated.
32 devices in a mesh: seq: 4 (over y, core), fsdp: 4 (over z), replica: 2 (over x).
Axes of the slice: x: 2, y: 2, z: 4, core: 2. Of those that a mesh axis runs over, the one named last changes fastest.
Arguments:
- inputs: bfloat16 [32, 1024, 768], P(('fsdp', 'replica'), 'seq'), may hold values from -6 to 6
- segments: int32 [32, 1024], P(('fsdp', 'replica')), may hold values from 0 to 15, as said below
- cotangent: bfloat16 [32, 1024, 768], P(('fsdp', 'replica'), 'seq'), may hold values from -6 to 6
- w_rows: float32 [768, 6144], P('fsdp')
- m_rows: float32 [768, 6144], P('fsdp')
- v_rows: float32 [768, 6144], P('fsdp')
- w_down: float32 [3072, 768], P('fsdp'), may hold values from -0.109375 to 0.109375
- m_down: float32 [3072, 768], P('fsdp')
- v_down: float32 [3072, 768], P('fsdp')
- smalls: float32 [12, 768], P(None, 'fsdp')
- m_small: float32 [12, 768], P(None, 'fsdp')
- v_small: float32 [12, 768], P(None, 'fsdp')
Outputs:
- activations: bfloat16 [32, 1024, 768], P(('fsdp', 'replica'), 'seq')
- input_grad: float32 [32, 1024, 768], P(('fsdp', 'replica'), 'seq')
- new_rows: float32 [768, 6144], P('fsdp')
- moment_rows: float32 [768, 6144], P('fsdp')
- second_rows: float32 [768, 6144], P('fsdp')
- new_down: float32 [3072, 768], P('fsdp')
- moment_down: float32 [3072, 768], P('fsdp')
- second_down: float32 [3072, 768], P('fsdp')
- new_small: float32 [12, 768], P(None, 'fsdp')
- moment_small: float32 [12, 768], P(None, 'fsdp')
- second_small: float32 [12, 768], P(None, 'fsdp')
Inputs may be any that keep to these rules, and one draw needn't show every extreme that they name: `segments`: in each sequence the document numbers start at 0, never fall and rise by at most one from a position to the next; every document but a sequence's last holds 64 to 800 positions; of the 4 sequences of one index pair of fsdp and replica, one is a single document; one sequence in all consists of 16 documents of 64 positions each.
All inputs are finite; a program needn't handle non-finite values.
Results may differ from a plain program's by a relative error of at most 0.023.
Values may be sent and summed in bfloat16 or wider, within the bound.
A program may use at most 320 MiB of HBM per device.

v0:
```python
import jax
import jax.numpy as jnp
from jax import lax
from jax.sharding import PartitionSpec as P

H = 12
STEP = 10


epsilon = 1e-05
beta_first = 0.9
beta_second = 0.999
adam_epsilon = 1e-08
weight_decay = 0.1
rate_rows = 0.08
rate_down = 0.04
rate_small = 0.5
masked_score = -1e30


def normalize(values, norm_gain, norm_shift):
    centered = values - jnp.mean(values, axis=-1, keepdims=True)
    spread = jnp.mean(centered * centered, axis=-1, keepdims=True)
    return centered * lax.rsqrt(spread + epsilon) * norm_gain + norm_shift


def smooth_gelu(values):
    return jax.nn.gelu(values, approximate=True)


def adam_update(weight, moment, second, gradient, step_rate, decay_rate):
    moment_new = beta_first * moment + (1.0 - beta_first) * gradient
    second_new = beta_second * second + (1.0 - beta_second) * gradient * gradient
    moment_hat = moment_new / (1.0 - beta_first**STEP)
    second_hat = second_new / (1.0 - beta_second**STEP)
    weight_new = weight - step_rate * (
        moment_hat / (jnp.sqrt(second_hat) + adam_epsilon) + decay_rate * weight
    )
    return (weight_new, moment_new, second_new)


def split_heads(values):
    return values.reshape(values.shape[0], values.shape[1], H, values.shape[2] // H)


def head_scores(query_heads, key_heads, allowed):
    score_scale = query_heads.shape[3] ** (-0.5)
    scores = (
        jnp.einsum("gqhe,gkhe->ghqk", query_heads, key_heads, preferred_element_type=jnp.float32)
        * score_scale
    )
    return jnp.where(allowed[:, None], scores, masked_score)


def attend(block_data):
    queries, keys_all, values_all, allowed = block_data
    scores = head_scores(split_heads(queries), split_heads(keys_all), allowed)
    largest = jnp.max(scores, axis=-1, keepdims=True)
    weights = jnp.exp(scores - largest)
    totals = jnp.sum(weights, axis=-1, keepdims=True)
    probabilities = (weights / totals).astype(jnp.bfloat16)
    attended = jnp.einsum(
        "ghqk,gkhe->gqhe",
        probabilities,
        split_heads(values_all),
        preferred_element_type=jnp.float32,
    )
    return (attended.reshape(queries.shape), largest + jnp.log(totals))


def attend_back(block_data):
    queries, keys_all, values_all, allowed, log_total, grad_attended = block_data
    query_heads = split_heads(queries)
    key_heads = split_heads(keys_all)
    value_heads = split_heads(values_all)
    grad_heads = split_heads(grad_attended)
    score_scale = query_heads.shape[3] ** (-0.5)
    probabilities = jnp.exp(head_scores(query_heads, key_heads, allowed) - log_total)
    grad_probs = jnp.einsum(
        "gqhe,gkhe->ghqk", grad_heads, value_heads, preferred_element_type=jnp.float32
    )
    grad_values = jnp.einsum(
        "ghqk,gqhe->gkhe",
        probabilities.astype(jnp.bfloat16),
        grad_heads,
        preferred_element_type=jnp.float32,
    )
    centered = jnp.sum(probabilities * grad_probs, axis=-1, keepdims=True)
    grad_scores = (probabilities * (grad_probs - centered)).astype(jnp.bfloat16)
    grad_queries = (
        jnp.einsum("ghqk,gkhe->gqhe", grad_scores, key_heads, preferred_element_type=jnp.float32)
        * score_scale
    )
    grad_keys = (
        jnp.einsum("ghqk,gqhe->gkhe", grad_scores, query_heads, preferred_element_type=jnp.float32)
        * score_scale
    )
    return (
        grad_queries.reshape(queries.shape),
        grad_keys.reshape(keys_all.shape),
        grad_values.reshape(keys_all.shape),
    )


def body(
    inputs,
    segments,
    cotangent,
    w_rows,
    m_rows,
    v_rows,
    w_down,
    m_down,
    v_down,
    smalls,
    m_small,
    v_small,
):
    seq_count, piece_rows, model_width = inputs.shape
    pair_count = seq_count // 2
    query_key_value_boundary = 3 * model_width
    output_boundary = 4 * model_width

    def paired(values):
        return values.reshape((pair_count, 2) + values.shape[1:])

    def unpaired(values):
        return values.reshape((seq_count,) + values.shape[2:])

    def over_tokens(values):
        return jnp.sum(values, axis=(0, 1))

    row_matrix_complete, down_matrix_complete, small_full = (
        lax.all_gather(w_rows.astype(jnp.bfloat16), "fsdp", axis=0, tiled=True),
        lax.all_gather(w_down.astype(jnp.bfloat16), "fsdp", axis=0, tiled=True),
        lax.all_gather(smalls.astype(jnp.bfloat16), "fsdp", axis=1, tiled=True),
    )
    small_vals = small_full.astype(jnp.float32)
    features = inputs.astype(jnp.float32)
    normed, norm_pull_one = jax.vjp(normalize, features, small_vals[0], small_vals[1])
    normalized_block = normed.astype(jnp.bfloat16)
    projected = jnp.einsum(
        "rxj,jw->rxw",
        normalized_block,
        row_matrix_complete[:, :query_key_value_boundary],
        preferred_element_type=jnp.float32,
    )
    queries = (projected[..., :model_width] + small_vals[2]).astype(jnp.bfloat16)
    keys_own = projected[..., model_width : 2 * model_width].astype(jnp.bfloat16)
    values_own = (projected[..., 2 * model_width :] + small_vals[3]).astype(jnp.bfloat16)
    keys_all, values_all = (
        lax.all_gather(keys_own, "seq", axis=1, tiled=True),
        lax.all_gather(values_own, "seq", axis=1, tiled=True),
    )
    offset = lax.axis_index("seq") * piece_rows
    query_segments = lax.dynamic_slice_in_dim(segments, offset, piece_rows, 1)
    query_places = offset + jnp.arange(piece_rows, dtype=jnp.int32)
    key_places = jnp.arange(segments.shape[1], dtype=jnp.int32)
    allowed = (query_places[:, None] >= key_places[None, :])[None] & (
        query_segments[:, :, None] == segments[:, None, :]
    )
    attended_pairs, log_total = lax.map(
        attend, (paired(queries), paired(keys_all), paired(values_all), paired(allowed))
    )
    attended_block = unpaired(attended_pairs).astype(jnp.bfloat16)
    residual = features + (
        jnp.einsum(
            "rxj,jw->rxw",
            attended_block,
            row_matrix_complete[:, query_key_value_boundary:output_boundary],
            preferred_element_type=jnp.float32,
        )
        + small_vals[4]
    )
    normed_two, norm_pull_two = jax.vjp(normalize, residual, small_vals[5], small_vals[6])
    second_normalized_block = normed_two.astype(jnp.bfloat16)
    hidden = jnp.einsum(
        "tyr,rw->tyw",
        second_normalized_block,
        row_matrix_complete[:, output_boundary:],
        preferred_element_type=jnp.float32,
    ) + small_vals[8:].reshape(-1)
    active, gelu_pull = jax.vjp(smooth_gelu, hidden)
    active_block = active.astype(jnp.bfloat16)
    activations = (
        residual
        + (
            jnp.einsum(
                "crx,xo->cro",
                active_block,
                down_matrix_complete,
                preferred_element_type=jnp.float32,
            )
            + small_vals[7]
        )
    ).astype(jnp.bfloat16)
    row_matrix_reverse, down_matrix_reverse = (
        lax.all_gather(w_rows.astype(jnp.bfloat16), "fsdp", axis=0, tiled=True),
        lax.all_gather(w_down.astype(jnp.bfloat16), "fsdp", axis=0, tiled=True),
    )
    upstream = cotangent.astype(jnp.float32)
    down_weight_gradient = jnp.einsum(
        "ezg,ezv->gv", active_block, cotangent, preferred_element_type=jnp.float32
    )
    grad_active = jnp.einsum(
        "tuy,qy->tuq", cotangent, down_matrix_reverse, preferred_element_type=jnp.float32
    )
    grad_hidden = gelu_pull(grad_active)[0]
    hidden_block_gradient = grad_hidden.astype(jnp.bfloat16)
    grad_up = jnp.einsum(
        "zng,znw->gw",
        second_normalized_block,
        hidden_block_gradient,
        preferred_element_type=jnp.float32,
    )
    grad_normed_two = jnp.einsum(
        "naz,ez->nae",
        hidden_block_gradient,
        row_matrix_reverse[:, output_boundary:],
        preferred_element_type=jnp.float32,
    )
    grad_residual_norm, grad_gain_two, grad_shift_two = norm_pull_two(grad_normed_two)
    grad_residual = upstream + grad_residual_norm
    residual_block_gradient = grad_residual.astype(jnp.bfloat16)
    grad_out_proj = jnp.einsum(
        "azk,azx->kx", attended_block, residual_block_gradient, preferred_element_type=jnp.float32
    )
    grad_attended_b = jnp.einsum(
        "wri,yi->wry",
        residual_block_gradient,
        row_matrix_reverse[:, query_key_value_boundary:output_boundary],
        preferred_element_type=jnp.float32,
    ).astype(jnp.bfloat16)
    query_pairs, key_pairs, value_pairs = lax.map(
        attend_back,
        (
            paired(queries),
            paired(keys_all),
            paired(values_all),
            paired(allowed),
            log_total,
            paired(grad_attended_b),
        ),
    )
    grad_queries = unpaired(query_pairs)
    grad_keys, grad_values = (
        lax.psum_scatter(
            unpaired(key_pairs).astype(jnp.bfloat16), "seq", scatter_dimension=1, tiled=True
        ).astype(jnp.float32),
        lax.psum_scatter(
            unpaired(value_pairs).astype(jnp.bfloat16), "seq", scatter_dimension=1, tiled=True
        ).astype(jnp.float32),
    )
    mixed_block_gradient = jnp.concatenate(
        [
            grad_queries.astype(jnp.bfloat16),
            grad_keys.astype(jnp.bfloat16),
            grad_values.astype(jnp.bfloat16),
        ],
        axis=-1,
    )
    query_key_value_gradient = jnp.einsum(
        "azk,azx->kx", normalized_block, mixed_block_gradient, preferred_element_type=jnp.float32
    )
    grad_normed = jnp.einsum(
        "wri,yi->wry",
        mixed_block_gradient,
        row_matrix_reverse[:, :query_key_value_boundary],
        preferred_element_type=jnp.float32,
    )
    grad_features, grad_gain_one, grad_shift_one = norm_pull_one(grad_normed)
    input_grad = grad_residual + grad_features
    grad_rows = jnp.concatenate([query_key_value_gradient, grad_out_proj, grad_up], axis=1)
    small_head = jnp.stack(
        [
            grad_gain_one,
            grad_shift_one,
            over_tokens(grad_queries),
            over_tokens(grad_values),
            over_tokens(grad_residual),
            grad_gain_two,
            grad_shift_two,
            over_tokens(upstream),
        ]
    )
    grad_small = jnp.concatenate(
        [small_head, over_tokens(grad_hidden).reshape(-1, model_width)], axis=0
    )
    shard_rows, shard_down, shard_small = (
        lax.psum_scatter(
            grad_rows.astype(jnp.bfloat16), "fsdp", scatter_dimension=0, tiled=True
        ).astype(jnp.float32),
        lax.psum_scatter(
            down_weight_gradient.astype(jnp.bfloat16), "fsdp", scatter_dimension=0, tiled=True
        ).astype(jnp.float32),
        lax.psum_scatter(
            grad_small.astype(jnp.bfloat16), "fsdp", scatter_dimension=1, tiled=True
        ).astype(jnp.float32),
    )
    total_rows, total_down, total_small = (
        lax.psum(shard_rows.astype(jnp.bfloat16), ("seq", "replica")).astype(jnp.float32),
        lax.psum(shard_down.astype(jnp.bfloat16), ("seq", "replica")).astype(jnp.float32),
        lax.psum(shard_small.astype(jnp.bfloat16), ("seq", "replica")).astype(jnp.float32),
    )
    new_rows, moment_rows, second_rows = adam_update(
        w_rows, m_rows, v_rows, total_rows, rate_rows, weight_decay
    )
    new_down, moment_down, second_down = adam_update(
        w_down, m_down, v_down, total_down, rate_down, weight_decay
    )
    new_small, moment_small, second_small = adam_update(
        smalls, m_small, v_small, total_small, rate_small, 0.0
    )
    return (
        activations,
        input_grad,
        new_rows,
        moment_rows,
        second_rows,
        new_down,
        moment_down,
        second_down,
        new_small,
        moment_small,
        second_small,
    )


def solution(mesh):
    in_specs = (
        P(("fsdp", "replica"), "seq", None),
        P(("fsdp", "replica"), None),
        P(("fsdp", "replica"), "seq", None),
        P("fsdp", None),
        P("fsdp", None),
        P("fsdp", None),
        P("fsdp", None),
        P("fsdp", None),
        P("fsdp", None),
        P(None, "fsdp"),
        P(None, "fsdp"),
        P(None, "fsdp"),
    )
    out_specs = (
        P(("fsdp", "replica"), "seq", None),
        P(("fsdp", "replica"), "seq", None),
        P("fsdp", None),
        P("fsdp", None),
        P("fsdp", None),
        P("fsdp", None),
        P("fsdp", None),
        P("fsdp", None),
        P(None, "fsdp"),
        P(None, "fsdp"),
        P(None, "fsdp"),
    )
    return jax.shard_map(body, mesh=mesh, in_specs=in_specs, out_specs=out_specs, check_vma=False)
```

profile of v0, /device:TPU:0, one launch (start us, length us, event | category | flops | bytes accessed | tf_op | source)
XLA Modules:
  0.0 1114.6 jit_solution(7503838375792285292)
XLA Ops:
  11.5 14.8 %all-gather = bf16[4,192,12]{1,2,0:T(8,128)(2,1)S(1)} all-gather(bf16[1,192,12]{1,2,0:T(8,128)(2,1)S(1)} %convert_bitcast_fusion), channel_id=1, replica_groups=mesh['seq'=4,'fsdp'=4,'replica'=2] {'fsdp'}, dimensions={0}, use_global_device_ids=true | all-gather | bytes 23040 | tf_op jit(solution)/shard_map/all_gather | solution.py:136
  28.0 153.1 %all-gather.6.cloned.1.call-done = bf16[768,6144]{1,0:T(8,128)(2,1)} async-done(((bf16[192,6144]{1,0:T(8,128)(2,1)}), bf16[768,6144]{1,0:T(8,128)(2,1)}) %all-gather.6.cloned.1.call-update) | async-done | bytes 9437200 | tf_op jit(solution)/shard_map/all_gather | solution.py:134
  201.8 34.9 %all-gather.8.cloned.1.call-done = bf16[4,1024,768]{2,1,0:T(8,128)(2,1)} async-done(((bf16[4,256,768]{2,1,0:T(8,128)(2,1)}), bf16[4,1024,768]{2,1,0:T(8,128)(2,1)}) %all-gather.8.cloned.1.call-update) | async-done | bytes 6291472 | tf_op jit(solution)/shard_map/all_gather | solution.py:153
  245.5 39.8 %all-gather.10.cloned.1.call-done = bf16[4,1024,768]{2,1,0:T(8,128)(2,1)} async-done(((bf16[4,256,768]{2,1,0:T(8,128)(2,1)}), bf16[4,1024,768]{2,1,0:T(8,128)(2,1)}) %all-gather.10.cloned.1.call-update) | async-done | bytes 6291472 | tf_op jit(solution)/shard_map/all_gather | solution.py:152
  294.0 78.3 %while.28 = (s32[]{:T(128)}, bf16[2,2,256,768]{2,3,1,0:T(8,128)(2,1)}, f32[2,2,12,256,1]{3,2,1,4,0:T(8,128)S(1)}, bf16[2,2,1024,768]{2,3,1,0:T(8,128)(2,1)}, pre...) while((s32[]{:T(128)}, ...), condition=%wide.region_5.6_spmd.clone, body=%wide.region_2.5_spmd.sunk.clone | while | flops 1686104064 | bytes 101933152 | solution.py:162
  298.2 10.6 fusion.130
  308.8 11.8 %fusion.131 = f32[2,12,256]{2,1,0:T(8,128)S(1)} fusion(f32[2,12,256,1024]{3,2,1,0:T(8,128)} %get-tuple-element.373, f32[2,12,256]{2,1,0:T(8,128)S(1)} %get-tuple-element.374, pred[2,256,1024]{2,1,0:T(8,128)(4,1)S(1)} %dynamic-slice_bitcast_fusion.9), kind=kLoop, calls=%fused_computation.4.clone.1.clone | loop fusion | flops 25159680 | bytes 25739264 | tf_op jit(solution)/shard_map/while/body/eval_jaxpr/reduce_sum | solution.py:60
  320.6 11.8 %fusion.132 = bf16[2,12,64,256]{3,2,1,0:T(8,128)(2,1)S(1)} fusion(bf16[2,1024,12,64]{1,3,2,0:T(8,128)(2,1)S(1)} %bitcast.191, f32[2,12,256,1024]{3,2,1,0:T(8,128)} %get-tuple-element.373, f32[2,12,256]{2,1,0:T(8,128)S(1)} %fusion.131, f32[2,12,256]{2,1,0:T(8,128)S(1)} %get-tuple-element.374, ...), kind=kOutput, calls=%fused_computation.5.clone.1.clone | convolution fusion | flops 836763648 | bytes 29671424 | tf_op jit(solution)/shard_map/while/body/eval_jaxpr/ghqk,gkhe->gqhe/dot_general | solution.py:62
  337.2 10.6 fusion.130
  347.8 11.8 %fusion.131 = f32[2,12,256]{2,1,0:T(8,128)S(1)} fusion(f32[2,12,256,1024]{3,2,1,0:T(8,128)} %get-tuple-element.373, f32[2,12,256]{2,1,0:T(8,128)S(1)} %get-tuple-element.374, pred[2,256,1024]{2,1,0:T(8,128)(4,1)S(1)} %dynamic-slice_bitcast_fusion.9), kind=kLoop, calls=%fused_computation.4.clone.1.clone | loop fusion | flops 25159680 | bytes 25739264 | tf_op jit(solution)/shard_map/while/body/eval_jaxpr/reduce_sum | solution.py:60
  359.6 11.7 %fusion.132 = bf16[2,12,64,256]{3,2,1,0:T(8,128)(2,1)S(1)} fusion(bf16[2,1024,12,64]{1,3,2,0:T(8,128)(2,1)S(1)} %bitcast.191, f32[2,12,256,1024]{3,2,1,0:T(8,128)} %get-tuple-element.373, f32[2,12,256]{2,1,0:T(8,128)S(1)} %fusion.131, f32[2,12,256]{2,1,0:T(8,128)S(1)} %get-tuple-element.374, ...), kind=kOutput, calls=%fused_computation.5.clone.1.clone | convolution fusion | flops 836763648 | bytes 29671424 | tf_op jit(solution)/shard_map/while/body/eval_jaxpr/ghqk,gkhe->gqhe/dot_general | solution.py:62
  386.3 17.4 %fusion.69 = (bf16[3072]{0:T(1024)(128)(2,1)}, bf16[4,256,3072]{2,1,0:T(8,128)(2,1)S(1)}) fusion(f32[4,256,3072]{2,1,0:T(8,128)} %fusion.30, f32[3072]{0:T(1024)S(1)} %copy-done.51, bf16[4,256,768]{2,1,0:T(8,128)(2,1)} %param.18, bf16[3072,768]{1,0:T(8,128)(2,1)} %all-gather.12.cloned.1.call-done), kind=kOutput, calls=%fused_computation.137 | convolution fusion | flops 4901041152 | bytes 25184256 | tf_op jit(solution)/shard_map/tuy,qy->tuq/dot_general | solution.py:205
  403.7 10.9 multiply_reduce_fusion.1
  421.9 189.5 %while.29 = (s32[]{:T(128)}, f32[2,2,256,768]{2,3,1,0:T(8,128)}, bf16[2,2,1024,768]{2,3,1,0:T(8,128)(2,1)}, bf16[2,2,1024,768]{2,3,1,0:T(8,128)(2,1)}, bf16[2,2,...) while((s32[]{:T(128)}, f32[2,2,256,768]{2,3,1,0:T(8,128)}, ...), condition=%wide.region_12.13_spmd.clone, body=%wide.region_10.12_spmd.sunk.clone | while | flops 4124436480 | bytes 340435392 | solution.py:234
  431.0 10.1 fusion.143
  441.1 12.5 %fusion.144 = bf16[2,12,64,1024]{3,2,1,0:T(8,128)(2,1)} fusion(bf16[2,256,12,64]{1,3,2,0:T(8,128)(2,1)S(1)} %bitcast.194, f32[2,12,256,1024]{3,2,1,0:T(8,128)} %fusion.143, f32[2,12,256]{2,1,0:T(8,128)S(1)} %dynamic-slice_bitcast_fusion.10, pred[2,256,1024]{2,1,0:T(8,128)(4,1)S(1)} %copy-done.3), kind=kOutput, calls=%fused_computation.18.clone.1.clone | convolution fusion | flops 830472192 | bytes 29646848 | tf_op jit(solution)/shard_map/while/body/eval_jaxpr/ghqk,gqhe->gkhe/dot_general | solution.py:82
  453.6 19.5 %multiply_reduce_fusion.6 = (f32[2,12,256]{2,1,0:T(8,128)S(1)}, f32[2,12,256,1024]{3,2,1,0:T(8,128)}) fusion(f32[2,12,256,1024]{3,2,1,0:T(8,128)} %fusion.143, f32[2,12,256]{2,1,0:T(8,128)S(1)} %dynamic-slice_bitcast_fusion.10, pred[2,256,1024]{2,1,0:T(8,128)(4,1)} %dynamic-slice_bitcast_fusion.11, bf16[2,256,12,64]{1,3,2,0:T(8,128)(2,1)} %bitcast.193, ...), kind=kOutput, calls=%fused_computation.15.clone.1.clone | convolution fusion | flops 836757504 | bytes 54837248 | tf_op jit(solution)/shard_map/while/body/eval_jaxpr/gqhe,gkhe->ghqk/dot_general | solution.py:79
  473.1 21.9 %multiply_convert_fusion.6 = bf16[2,12,256,1024]{3,2,1,0:T(8,128)(2,1)} fusion(f32[2,12,256,1024]{3,2,1,0:T(8,128)} %get-tuple-element.394, f32[2,12,256,1024]{3,2,1,0:T(8,128)} %fusion.143, f32[2,12,256]{2,1,0:T(8,128)S(1)} %get-tuple-element.395, f32[2,12,256]{2,1,0:T(8,128)S(1)} %dynamic-slice_bitcast_fusion.10, ...), kind=kLoop, calls=%fused_computation.14.clone.1.clone | loop fusion | flops 37748736 | bytes 63488000 | tf_op jit(solution)/shard_map/while/body/eval_jaxpr/convert_element_type | solution.py:89
  525.5 10.1 fusion.143
  535.6 12.5 %fusion.144 = bf16[2,12,64,1024]{3,2,1,0:T(8,128)(2,1)} fusion(bf16[2,256,12,64]{1,3,2,0:T(8,128)(2,1)S(1)} %bitcast.194, f32[2,12,256,1024]{3,2,1,0:T(8,128)} %fusion.143, f32[2,12,256]{2,1,0:T(8,128)S(1)} %dynamic-slice_bitcast_fusion.10, pred[2,256,1024]{2,1,0:T(8,128)(4,1)S(1)} %copy-done.3), kind=kOutput, calls=%fused_computation.18.clone.1.clone | convolution fusion | flops 830472192 | bytes 29646848 | tf_op jit(solution)/shard_map/while/body/eval_jaxpr/ghqk,gqhe->gkhe/dot_general | solution.py:82
  548.1 19.5 %multiply_reduce_fusion.6 = (f32[2,12,256]{2,1,0:T(8,128)S(1)}, f32[2,12,256,1024]{3,2,1,0:T(8,128)}) fusion(f32[2,12,256,1024]{3,2,1,0:T(8,128)} %fusion.143, f32[2,12,256]{2,1,0:T(8,128)S(1)} %dynamic-slice_bitcast_fusion.10, pred[2,256,1024]{2,1,0:T(8,128)(4,1)} %dynamic-slice_bitcast_fusion.11, bf16[2,256,12,64]{1,3,2,0:T(8,128)(2,1)} %bitcast.193, ...), kind=kOutput, calls=%fused_computation.15.clone.1.clone | convolution fusion | flops 836757504 | bytes 54837248 | tf_op jit(solution)/shard_map/while/body/eval_jaxpr/gqhe,gkhe->ghqk/dot_general | solution.py:79
  567.6 21.9 %multiply_convert_fusion.6 = bf16[2,12,256,1024]{3,2,1,0:T(8,128)(2,1)} fusion(f32[2,12,256,1024]{3,2,1,0:T(8,128)} %get-tuple-element.394, f32[2,12,256,1024]{3,2,1,0:T(8,128)} %fusion.143, f32[2,12,256]{2,1,0:T(8,128)S(1)} %get-tuple-element.395, f32[2,12,256]{2,1,0:T(8,128)S(1)} %dynamic-slice_bitcast_fusion.10, ...), kind=kLoop, calls=%fused_computation.14.clone.1.clone | loop fusion | flops 37748736 | bytes 63488000 | tf_op jit(solution)/shard_map/while/body/eval_jaxpr/convert_element_type | solution.py:89
  620.2 8.8 copy.68
  630.8 12.5 %bitcast_convert_fusion = bf16[3072,768]{1,0:T(8,128)(2,1)} fusion(bf16[4,256,768]{2,1,0:T(8,128)(2,1)S(1)} %copy-done.15, f32[4,256,3072]{2,1,0:T(8,128)} %fusion.30, f32[3072]{0:T(1024)S(1)} %copy-done.52), kind=kOutput, calls=%fused_computation.43 | convolution fusion | flops 4865654784 | bytes 18886656 | tf_op jit(solution)/shard_map/ezg,ezv->gv/dot_general | solution.py:202
  655.9 10.5 bitcast_convert_fusion.1
  666.3 12.3 %reduce-scatter.10.cloned.1.call-done = bf16[4,256,768]{2,1,0:T(8,128)(2,1)} async-done(((bf16[4,1024,768]{2,1,0:T(8,128)(2,1)}), bf16[4,256,768]{2,1,0:T(8,128)(2,1)}) %reduce-scatter.10.cloned.1.call-update) | async-done | bytes 1572880 | tf_op jit(solution)/shard_map/reduce_scatter | solution.py:250
  678.6 61.0 %reduce-scatter.8.cloned.1.call-done = bf16[4,256,768]{2,1,0:T(8,128)(2,1)} async-done(((bf16[4,1024,768]{2,1,0:T(8,128)(2,1)}), bf16[4,256,768]{2,1,0:T(8,128)(2,1)}) %reduce-scatter.8.cloned.1.call-update) | async-done | bytes 1572880 | tf_op jit(solution)/shard_map/reduce_scatter | solution.py:247
  764.3 63.5 %reduce-scatter.14.cloned.1.call-done = bf16[768,768]{1,0:T(8,128)(2,1)} async-done(((bf16[3072,768]{1,0:T(8,128)(2,1)}), bf16[768,768]{1,0:T(8,128)(2,1)}) %reduce-scatter.14.cloned.1.call-update) | async-done | bytes 1179664 | tf_op jit(solution)/shard_map/reduce_scatter | solution.py:293
  827.7 164.2 %reduce-scatter.12.cloned.1.call-done = bf16[192,6144]{1,0:T(8,128)(2,1)} async-done(((bf16[768,6144]{1,0:T(8,128)(2,1)}), bf16[192,6144]{1,0:T(8,128)(2,1)}) %reduce-scatter.12.cloned.1.call-update) | async-done | bytes 2359312 | tf_op jit(solution)/shard_map/reduce_scatter | solution.py:290
  992.0 13.8 %add_convert_fusion = bf16[4,256,768]{2,1,0:T(8,128)(2,1)} fusion(f32[4,256,768]{2,1,0:T(8,128)} %copy-done.17, bf16[3072,768]{1,0:T(8,128)(2,1)} %all-gather.12.cloned.1.call-done, f32[768]{0:T(1024)S(1)} %copy-done.55, f32[4,256,3072]{2,1,0:T(8,128)} %fusion.30, f32[3072]{0:T(1024)S(1)} %copy-done.52), kind=kOutput, calls=%fused_computation.89 | convolution fusion | flops 4865654784 | bytes 22035456 | tf_op jit(solution)/shard_map/crx,xo->cro/dot_general | solution.py:188
  1015.9 14.2 %psum.23 = bf16[12,192]{1,0:T(8,128)(2,1)S(1)} all-reduce(bf16[12,192]{1,0:T(8,128)(2,1)S(1)} %copy.83), channel_id=1, replica_groups=mesh['seq'=4,'fsdp'=4,'replica'=2] {'seq','replica'}, use_global_device_ids=true, to_apply=%region_31.32 | all-reduce | flops 2304 | bytes 9216 | tf_op jit(solution)/shard_map/psum | solution.py:303
  1030.8 60.4 %all-reduce.3.cloned.1.call-done = (bf16[192,6144]{1,0:T(8,128)(2,1)}, bf16[768,768]{1,0:T(8,128)(2,1)}) async-done(((bf16[192,6144]{1,0:T(8,128)(2,1)}, bf16[768,768]{1,0:T(8,128)(2,1)}), (bf16[192,6144]{1,0:T(8,128)(2,1)}, bf16[768,768]{1,0:T(8,128)(2,1)})) %all-reduce.3.cloned.1.call-update) | async-done | bytes 3538960 | tf_op jit(solution)/shard_map/psum | solution.py:301
  (281 shorter events, 210.3 us)
Async XLA Ops:
  7.2 19.9 %copy-start.12 = (bf16[4,256,768]{2,1,0:T(8,128)(2,1)S(1)}, bf16[4,256,768]{2,1,0:T(8,128)(2,1)}, u32[]{:S(2)}) copy-start(bf16[4,256,768]{2,1,0:T(8,128)(2,1)} %param.16) | copy-start | bytes 4718596
  7.2 173.9 %all-gather.6.cloned.1.call-start = ((), (), s32[]{:S(2)}) async-start(), calls=%async_computation.5 | async-start | bytes 11796480 | tf_op jit(solution)/shard_map/all_gather | solution.py:134
  11.4 225.3 %all-gather.8.cloned.1.call-start = ((), (), s32[]{:S(2)}) async-start(), calls=%async_computation.6 | async-start | bytes 7864320 | tf_op jit(solution)/shard_map/all_gather | solution.py:153
  27.1 160.1 %copy-start.34 = (f32[768]{0:T(1024)}, f32[768]{0:T(1024)S(1)}, u32[]{:S(2)}) copy-start(f32[768]{0:T(1024)S(1)} %get-tuple-element.173) | copy-start | bytes 9220
  27.1 160.2 %copy-start.56 = (f32[768]{0:T(1024)}, f32[768]{0:T(1024)S(1)}, u32[]{:S(2)}) copy-start(f32[768]{0:T(1024)S(1)} %get-tuple-element.172) | copy-start | bytes 9220
  27.4 159.9 %copy-start.30 = (f32[4,256]{1,0:T(4,128)}, f32[4,256]{1,0:T(4,128)S(1)}, u32[]{:S(2)}) copy-start(f32[4,256]{1,0:T(4,128)S(1)} %broadcast_multiply_fusion.2) | copy-start | bytes 12292
  27.9 159.3 %copy-start.42 = (f32[4,256]{1,0:T(4,128)}, f32[4,256]{1,0:T(4,128)S(1)}, u32[]{:S(2)}) copy-start(f32[4,256]{1,0:T(4,128)S(1)} %fusion.36) | copy-start | bytes 12292
  28.0 159.3 %copy-start.36 = (f32[4,256]{1,0:T(4,128)}, f32[4,256]{1,0:T(4,128)S(1)}, u32[]{:S(2)}) copy-start(f32[4,256]{1,0:T(4,128)S(1)} %fusion.55) | copy-start | bytes 12292
  192.0 93.3 %all-gather.10.cloned.1.call-start = ((), (), s32[]{:S(2)}) async-start(), calls=%async_computation.7 | async-start | bytes 7864320 | tf_op jit(solution)/shard_map/all_gather | solution.py:152
  195.4 190.8 %all-gather.12.cloned.1.call-start = ((), (), s32[]{:S(2)}) async-start(), calls=%async_computation.8 | async-start | bytes 5898240 | tf_op jit(solution)/shard_map/all_gather | solution.py:135
  196.6 482.0 %reduce-scatter.10.cloned.1.call-start = ((), (), s32[]{:S(2)}) async-start(), calls=%async_computation.10 | async-start | bytes 7864320 | tf_op jit(solution)/shard_map/reduce_scatter | solution.py:250
  294.0 78.3 %copy-start.60 = (f32[768]{0:T(1024)S(1)}, f32[768]{0:T(1024)}, u32[]{:S(2)}) copy-start(f32[768]{0:T(1024)} %get-tuple-element.169) | copy-start | bytes 9220
  376.3 38.2 %copy-start.40 = (f32[4,256]{1,0:T(4,128)}, f32[4,256]{1,0:T(4,128)S(1)}, u32[]{:S(2)}) copy-start(f32[4,256]{1,0:T(4,128)S(1)} %broadcast_multiply_fusion.1) | copy-start | bytes 12292
  376.9 37.7 %copy-start.47 = (f32[4,256]{1,0:T(4,128)}, f32[4,256]{1,0:T(4,128)S(1)}, u32[]{:S(2)}) copy-start(f32[4,256]{1,0:T(4,128)S(1)} %fusion.56) | copy-start | bytes 12292
  386.2 17.4 %copy-start.18 = (f32[4,256,768]{2,1,0:T(8,128)S(1)}, f32[4,256,768]{2,1,0:T(8,128)}, u32[]{:S(2)}) copy-start(f32[4,256,768]{2,1,0:T(8,128)} %copy-done.17) | copy-start | bytes 9437188
  620.1 119.4 %reduce-scatter.8.cloned.1.call-start = ((), (), s32[]{:S(2)}) async-start(), calls=%async_computation.9 | async-start | bytes 7864320 | tf_op jit(solution)/shard_map/reduce_scatter | solution.py:247
  629.0 198.8 %reduce-scatter.14.cloned.1.call-start = ((), (), s32[]{:S(2)}) async-start(), calls=%async_computation.12 | async-start | bytes 5898240 | tf_op jit(solution)/shard_map/reduce_scatter | solution.py:293
  643.3 348.6 %reduce-scatter.12.cloned.1.call-start = ((), (), s32[]{:S(2)}) async-start(), calls=%async_computation.11 | async-start | bytes 11796480 | tf_op jit(solution)/shard_map/reduce_scatter | solution.py:290
  655.8 83.8 %copy-start.13 = (bf16[4,256,768]{2,1,0:T(8,128)(2,1)S(1)}, bf16[4,256,768]{2,1,0:T(8,128)(2,1)}, u32[]{:S(2)}) copy-start(bf16[4,256,768]{2,1,0:T(8,128)(2,1)} %param.16) | copy-start | bytes 4718596
  655.8 83.7 %copy-start.31 = (f32[4,256]{1,0:T(4,128)S(1)}, f32[4,256]{1,0:T(4,128)}, u32[]{:S(2)}) copy-start(f32[4,256]{1,0:T(4,128)} %copy-done.30) | copy-start | bytes 12292
  655.8 83.7 %copy-start.35 = (f32[768]{0:T(1024)S(1)}, f32[768]{0:T(1024)}, u32[]{:S(2)}) copy-start(f32[768]{0:T(1024)} %copy-done.34) | copy-start | bytes 9220
  655.8 83.7 %copy-start.37 = (f32[4,256]{1,0:T(4,128)S(1)}, f32[4,256]{1,0:T(4,128)}, u32[]{:S(2)}) copy-start(f32[4,256]{1,0:T(4,128)} %copy-done.36) | copy-start | bytes 12292
  655.8 83.7 %copy-start.57 = (f32[768]{0:T(1024)S(1)}, f32[768]{0:T(1024)}, u32[]{:S(2)}) copy-start(f32[768]{0:T(1024)} %copy-done.56) | copy-start | bytes 9220
  750.5 264.5 %reduce-scatter.16.cloned.1.call-start = ((), (), s32[]{:S(2)}) async-start(), calls=%async_computation.13 | async-start | bytes 245760
  763.3 228.7 %copy-start.55 = (f32[768]{0:T(1024)S(1)}, f32[768]{0:T(1024)}, u32[]{:S(2)}) copy-start(f32[768]{0:T(1024)} %get-tuple-element.167) | copy-start | bytes 9220
  764.2 326.9 %all-reduce.3.cloned.1.call-start = ((), (), s32[]{:S(2)}) async-start(), calls=%async_computation.14 | async-start | bytes 7077888 | tf_op jit(solution)/shard_map/psum | solution.py:301
  992.0 13.8 %copy-start.11 = (f32[4,256,768]{2,1,0:T(8,128)S(1)}, f32[4,256,768]{2,1,0:T(8,128)}, u32[]{:S(2)}) copy-start(f32[4,256,768]{2,1,0:T(8,128)} %copy-done.10) | copy-start | bytes 9437188
  992.0 13.8 %copy-start.16 = (bf16[4,256,768]{2,1,0:T(8,128)(2,1)S(1)}, bf16[4,256,768]{2,1,0:T(8,128)(2,1)}, u32[]{:S(2)}) copy-start(bf16[4,256,768]{2,1,0:T(8,128)(2,1)} %param.18) | copy-start | bytes 4718596
  1005.8 24.3 %copy-start.33 = (f32[12,192]{1,0:T(8,128)S(1)}, f32[12,192]{1,0:T(8,128)}, u32[]{:S(2)}) copy-start(f32[12,192]{1,0:T(8,128)} %param.25) | copy-start | bytes 27652
  1005.8 24.3 %copy-start.49 = (f32[12,192]{1,0:T(8,128)S(1)}, f32[12,192]{1,0:T(8,128)}, u32[]{:S(2)}) copy-start(f32[12,192]{1,0:T(8,128)} %param.26) | copy-start | bytes 27652
  1005.8 24.3 %copy-start.50 = (f32[12,192]{1,0:T(8,128)S(1)}, f32[12,192]{1,0:T(8,128)}, u32[]{:S(2)}) copy-start(f32[12,192]{1,0:T(8,128)} %param.27) | copy-start | bytes 27652
  1005.9 93.0 %slice-start = ((s8[4718592]{0:T(1024)(128)(4,1)}), s8[524288]{0:T(1024)(128)(4,1)S(1)}, s32[]{:S(2)}) async-start(s8[4718592]{0:T(1024)(128)(4,1)} %bitcast.198), calls=%async_computation.15 | async-start | bytes 1048576
  (57 other events, 297.9 us)
Sparse Core Ops, SparseCore 0:
  11.6 169.4 all-gather.5
  192.1 44.5 all-gather.7
  238.9 46.3 all-gather.9
  287.3 89.4 all-gather.11
  620.2 58.3 reduce-scatter.9
  681.2 58.3 reduce-scatter.7
  742.4 85.2 reduce-scatter.13
  830.1 161.8 reduce-scatter.11
  994.8 20.1 reduce-scatter.15
  1018.6 72.4 all-reduce.2
where the time goes:
time: 1120 us; the launch traced here: 1110 us
  waiting for transfers between devices  596 us (53%)
  matrix products  266 us (24%)
  other arithmetic  113 us (10%)
  local copies, waits for them, and re-layouts  95.3 us (9%)
  blocking collectives  29 us (3%)
  between operations  15.1 us (1%)
    reduce_scatter x1, waiting for transfers between devices, body(): lax.psum_scatter(grad_rows.astype(jnp.bfloat16), 'fsdp', scatter_dimensio...  164 us
    all_gather x1, waiting for transfers between devices, body(): lax.all_gather(w_rows.astype(jnp.bfloat16), 'fsdp', axis=0, tiled=True)  153 us
    reduce_scatter x1, waiting for transfers between devices, body(): lax.psum_scatter(down_weight_gradient.astype(jnp.bfloat16), 'fsdp', scatt...  63.5 us
    reduce_scatter x1, waiting for transfers between devices, body(): lax.psum_scatter(unpaired(key_pairs).astype(jnp.bfloat16), 'seq', scatter...  61 us
    psum x1, waiting for transfers between devices, body(): lax.psum(shard_rows.astype(jnp.bfloat16), ('seq', 'replica'))  60.4 us
    convert_element_type x2, other arithmetic, attend_back(): grad_scores = (probabilities * (grad_probs - centered)).astype(jnp.bfloat16)  43.8 us
    dot_general x4, matrix products, head_scores(): jnp.einsum('gqhe,gkhe->ghqk', query_heads, key_heads, preferred_element_t...  41.4 us
    all_gather x1, waiting for transfers between devices, body(): lax.all_gather(keys_own, 'seq', axis=1, tiled=True)  39.8 us
  transfers between devices with their start and end apart: 10, of which 9 were waited for; matrix products, arithmetic and copies ran while one was open for 18% of the time, Pallas kernels for 0%

commit v1 on v0

v1 whole, which is shorter than its diff:
```python
import functools

import jax
import jax.numpy as jnp
from jax import lax
from jax.experimental import pallas as pl
from jax.experimental.pallas import tpu as pltpu
from jax.sharding import PartitionSpec as P

H = 12
STEP = 10


epsilon = 1e-05
beta_first = 0.9
beta_second = 0.999
adam_epsilon = 1e-08
weight_decay = 0.1
rate_rows = 0.08
rate_down = 0.04
rate_small = 0.5
masked_score = -1e30


def normalize(values, norm_gain, norm_shift):
    centered = values - jnp.mean(values, axis=-1, keepdims=True)
    spread = jnp.mean(centered * centered, axis=-1, keepdims=True)
    return centered * lax.rsqrt(spread + epsilon) * norm_gain + norm_shift


def smooth_gelu(values):
    return jax.nn.gelu(values, approximate=True)


def adam_update(weight, moment, second, gradient, step_rate, decay_rate):
    moment_new = beta_first * moment + (1.0 - beta_first) * gradient
    second_new = beta_second * second + (1.0 - beta_second) * gradient * gradient
    moment_hat = moment_new / (1.0 - beta_first**STEP)
    second_hat = second_new / (1.0 - beta_second**STEP)
    weight_new = weight - step_rate * (
        moment_hat / (jnp.sqrt(second_hat) + adam_epsilon) + decay_rate * weight
    )
    return (weight_new, moment_new, second_new)


LANES = 128
BLOCK = 256


def lane_masks(head_width):
    lane = lax.broadcasted_iota(jnp.int32, (1, LANES), 1)
    return [
        ((lane >= start) & (lane < start + head_width)).astype(jnp.float32).astype(jnp.bfloat16)
        for start in range(0, LANES, head_width)
    ]


def transposed(values):
    return values.astype(jnp.float32).T.astype(jnp.bfloat16)


def dot_lanes(left, right):
    return lax.dot_general(
        left, right, (((1,), (1,)), ((), ())), preferred_element_type=jnp.float32
    )


def dot_plain(left, right):
    return jnp.dot(left, right, preferred_element_type=jnp.float32)


def mask_bias(places_col, places_row, start, stop):
    key_segments = places_col[:stop]
    query_segments = places_row[:, start:stop]
    key_places = lax.broadcasted_iota(jnp.int32, (stop, stop - start), 0)
    query_places = start + lax.broadcasted_iota(jnp.int32, (stop, stop - start), 1)
    allowed = (key_segments == query_segments) & (key_places <= query_places)
    return jnp.where(allowed, 0.0, masked_score)


def attend_kernel(head_width, q_ref, k_ref, v_ref, row_ref, col_ref, out_ref):
    length = q_ref.shape[1]
    keys = k_ref[0]
    values_t = transposed(v_ref[0])
    masks = lane_masks(head_width)
    scale = head_width ** (-0.5)
    for start in range(0, length, BLOCK):
        stop = start + BLOCK
        bias = mask_bias(col_ref[0], row_ref[0], start, stop)
        queries = q_ref[0, start:stop, :] * jnp.bfloat16(scale)
        parts = []
        for head, mask in enumerate(masks):
            scores = dot_lanes(keys[:stop], queries * mask) + bias
            largest = jnp.max(scores, axis=0, keepdims=True)
            weights = jnp.exp(scores - largest)
            totals = jnp.sum(weights, axis=0, keepdims=True)
            low = head * head_width
            mixed = dot_plain(
                values_t[low : low + head_width, :stop], weights.astype(jnp.bfloat16)
            )
            parts.append(mixed / totals)
        out_ref[0, start:stop, :] = jnp.concatenate(parts, axis=0).T.astype(jnp.bfloat16)


def attend_back_kernel(
    head_width, q_ref, k_ref, v_ref, g_ref, row_ref, col_ref, dq_ref, dk_ref, dv_ref, dk_sum, dv_sum
):
    length = q_ref.shape[1]
    keys = k_ref[0]
    values = v_ref[0]
    keys_t = transposed(keys)
    masks = lane_masks(head_width)
    scale = head_width ** (-0.5)
    dk_sum[...] = jnp.zeros_like(dk_sum)
    dv_sum[...] = jnp.zeros_like(dv_sum)
    for start in range(0, length, BLOCK):
        stop = start + BLOCK
        bias = mask_bias(col_ref[0], row_ref[0], start, stop)
        queries = q_ref[0, start:stop, :] * jnp.bfloat16(scale)
        grads = g_ref[0, start:stop, :]
        dq_parts, probs_parts, ds_parts = [], [], []
        query_heads = [queries * mask for mask in masks]
        grad_heads = [grads * mask for mask in masks]
        for head in range(len(masks)):
            scores = dot_lanes(keys[:stop], query_heads[head]) + bias
            largest = jnp.max(scores, axis=0, keepdims=True)
            weights = jnp.exp(scores - largest)
            totals = jnp.sum(weights, axis=0, keepdims=True)
            probs = weights * (1.0 / totals)
            grad_probs = dot_lanes(values[:stop], grad_heads[head])
            centered = jnp.sum(probs * grad_probs, axis=0, keepdims=True)
            grad_scores = (probs * (grad_probs - centered)).astype(jnp.bfloat16)
            low = head * head_width
            dq_parts.append(dot_plain(keys_t[low : low + head_width, :stop], grad_scores))
            ds_parts.append(grad_scores)
            probs_parts.append(probs.astype(jnp.bfloat16))
        dk_sum[:stop, :] += dot_plain(
            jnp.concatenate(ds_parts, axis=1), jnp.concatenate(query_heads, axis=0)
        )
        dv_sum[:stop, :] += dot_plain(
            jnp.concatenate(probs_parts, axis=1), jnp.concatenate(grad_heads, axis=0)
        )
        dq = jnp.concatenate(dq_parts, axis=0) * scale
        dq_ref[0, start:stop, :] = dq.T.astype(jnp.bfloat16)
    dk_ref[0] = dk_sum[...].astype(jnp.bfloat16)
    dv_ref[0] = dv_sum[...].astype(jnp.bfloat16)


def attention_specs(length, groups):
    def column(offset):
        return pl.BlockSpec((1, length, LANES), lambda n, j: (n, 0, offset * groups + j))

    row = pl.BlockSpec((1, 1, length), lambda n, j: (n, 0, 0))
    col = pl.BlockSpec((1, length, 1), lambda n, j: (n, 0, 0))
    return column, row, col


def attend(mixed, rows, cols):
    count, length, width = mixed.shape
    width //= 3
    groups = width // LANES
    column, row, col = attention_specs(length, groups)
    return pl.pallas_call(
        functools.partial(attend_kernel, width // H),
        grid=(count, groups),
        in_specs=[column(0), column(1), column(2), row, col],
        out_specs=column(0),
        out_shape=jax.ShapeDtypeStruct((count, length, width), jnp.bfloat16),
        compiler_params=pltpu.CompilerParams(vmem_limit_bytes=48 * 2**20),
        cost_estimate=pl.CostEstimate(
            flops=3 * count * length * length * width,
            bytes_accessed=8 * count * length * width,
            transcendentals=count * H * length * length // 2,
        ),
    )(mixed, mixed, mixed, rows, cols)


def attend_back(mixed, grads, rows, cols):
    count, length, width = grads.shape
    groups = width // LANES
    column, row, col = attention_specs(length, groups)
    shape = jax.ShapeDtypeStruct((count, length, width), jnp.bfloat16)
    return pl.pallas_call(
        functools.partial(attend_back_kernel, width // H),
        grid=(count, groups),
        in_specs=[column(0), column(1), column(2), column(0), row, col],
        out_specs=[column(0)] * 3,
        out_shape=[shape] * 3,
        scratch_shapes=[pltpu.VMEM((length, LANES), jnp.float32)] * 2,
        compiler_params=pltpu.CompilerParams(vmem_limit_bytes=48 * 2**20),
        cost_estimate=pl.CostEstimate(
            flops=7 * count * length * length * width,
            bytes_accessed=14 * count * length * width,
            transcendentals=count * H * length * length // 2,
        ),
    )(mixed, mixed, mixed, grads, rows, cols)


def partner(values, axis, bit):
    size = lax.axis_size(axis)
    return lax.ppermute(values, axis, [(i, i ^ bit) for i in range(size)])


def half_of(values, upper, dim):
    half = values.shape[dim] // 2
    return lax.dynamic_slice_in_dim(values, upper * half, half, dim)


def gather_columns(values, extra=None):
    upper = lax.axis_index("seq") & 1
    own = half_of(values, upper, 1)
    width = own.shape[1]
    if extra is not None:
        own = jnp.concatenate([own, extra], axis=1)
    full = lax.all_gather(own, "fsdp", axis=0, tiled=True)
    mine = full[:, :width]
    other = partner(mine, "seq", 1)
    first = upper == 0
    whole = jnp.concatenate(
        [jnp.where(first, mine, other), jnp.where(first, other, mine)], axis=1
    )
    return whole, full[:, width:]


def halve(values, axis, bit, dim):
    upper = (lax.axis_index(axis) // bit) & 1
    kept = half_of(values, upper, dim)
    got = partner(half_of(values, 1 - upper, dim), axis, bit)
    return (kept.astype(jnp.float32) + got.astype(jnp.float32)).astype(jnp.bfloat16)


def plane_steps():
    seq_bits = [("seq", 1 << i) for i in range(lax.axis_size("seq").bit_length() - 1)]
    replica_bits = [("replica", 1 << i) for i in range(lax.axis_size("replica").bit_length() - 1)]
    return seq_bits[:1], seq_bits[1:], replica_bits


def reduce_to_owner(values, dim, seq_first):
    shards = lax.axis_size("fsdp")
    values = values.astype(jnp.bfloat16)
    values = values.reshape((shards, values.shape[0] // shards) + values.shape[1:])
    cut = 2 if dim == 1 else 1
    first, rest, replicas = plane_steps()
    steps = first + (rest + replicas if seq_first else replicas + rest)
    for axis, bit in steps:
        values = halve(values, axis, bit, cut)
    values = lax.psum_scatter(values, "fsdp", scatter_dimension=0, tiled=False)
    return values, steps


def collect(values, steps, dim):
    for axis, bit in reversed(steps):
        upper = (lax.axis_index(axis) // bit) & 1
        other = partner(values, axis, bit)
        first = upper == 0
        values = jnp.concatenate(
            [jnp.where(first, values, other), jnp.where(first, other, values)], axis=dim
        )
    return values


def owner_sum(values, dim, seq_first):
    part, steps = reduce_to_owner(values, dim, seq_first)
    return collect(part, steps, dim).astype(jnp.float32)


def body(
    inputs,
    segments,
    cotangent,
    w_rows,
    m_rows,
    v_rows,
    w_down,
    m_down,
    v_down,
    smalls,
    m_small,
    v_small,
):
    seq_count, piece_rows, model_width = inputs.shape
    query_key_value_boundary = 3 * model_width
    small_rows = smalls.shape[0]

    def over_tokens(values):
        return jnp.sum(values, axis=(0, 1))

    rows_b = w_rows.astype(jnp.bfloat16)
    small_pad = jnp.pad(smalls.astype(jnp.bfloat16).T, ((0, 0), (0, LANES - small_rows)))
    matrix_qkv, small_full = gather_columns(rows_b[:, :query_key_value_boundary], small_pad)
    rows_rest, down_b, matrix_qkv, small_full = lax.optimization_barrier(
        (
            rows_b[:, query_key_value_boundary:],
            w_down.astype(jnp.bfloat16),
            matrix_qkv,
            small_full,
        )
    )
    matrix_rest, _ = gather_columns(rows_rest)
    matrix_down, _ = gather_columns(down_b)
    matrix_out = matrix_rest[:, :model_width]
    matrix_up = matrix_rest[:, model_width:]
    small_vals = small_full[:, :small_rows].T.astype(jnp.float32)
    features = inputs.astype(jnp.float32)
    normed, norm_pull_one = jax.vjp(normalize, features, small_vals[0], small_vals[1])
    normalized_block = normed.astype(jnp.bfloat16)
    projected = jnp.einsum(
        "rxj,jw->rxw", normalized_block, matrix_qkv, preferred_element_type=jnp.float32
    )
    bias = jnp.concatenate([small_vals[2], jnp.zeros_like(small_vals[2]), small_vals[3]])
    mixed = lax.all_to_all(
        (projected + bias).astype(jnp.bfloat16), "seq", split_axis=0, concat_axis=1, tiled=True
    )
    own_count = mixed.shape[0]
    own_segments = lax.dynamic_slice_in_dim(
        segments, lax.axis_index("seq") * own_count, own_count, 0
    )
    segment_rows = own_segments[:, None, :]
    segment_cols = own_segments[:, :, None]
    attended_block = lax.all_to_all(
        attend(mixed, segment_rows, segment_cols), "seq", split_axis=1, concat_axis=0, tiled=True
    )
    residual = features + (
        jnp.einsum(
            "rxj,jw->rxw",
            attended_block,
            matrix_out,
            preferred_element_type=jnp.float32,
        )
        + small_vals[4]
    )
    normed_two, norm_pull_two = jax.vjp(normalize, residual, small_vals[5], small_vals[6])
    second_normalized_block = normed_two.astype(jnp.bfloat16)
    hidden = jnp.einsum(
        "tyr,rw->tyw",
        second_normalized_block,
        matrix_up,
        preferred_element_type=jnp.float32,
    ) + small_vals[8:].reshape(-1)
    active, gelu_pull = jax.vjp(smooth_gelu, hidden)
    active_block = active.astype(jnp.bfloat16)
    activations = (
        residual
        + (
            jnp.einsum(
                "crx,xo->cro",
                active_block,
                matrix_down,
                preferred_element_type=jnp.float32,
            )
            + small_vals[7]
        )
    ).astype(jnp.bfloat16)
    upstream = cotangent.astype(jnp.float32)
    down_weight_gradient = jnp.einsum(
        "ezg,ezv->gv", active_block, cotangent, preferred_element_type=jnp.float32
    )
    grad_active = jnp.einsum(
        "tuy,qy->tuq", cotangent, matrix_down, preferred_element_type=jnp.float32
    )
    grad_hidden = gelu_pull(grad_active)[0]
    hidden_block_gradient = grad_hidden.astype(jnp.bfloat16)
    grad_up = jnp.einsum(
        "zng,znw->gw",
        second_normalized_block,
        hidden_block_gradient,
        preferred_element_type=jnp.float32,
    )
    grad_normed_two = jnp.einsum(
        "naz,ez->nae",
        hidden_block_gradient,
        matrix_up,
        preferred_element_type=jnp.float32,
    )
    grad_residual_norm, grad_gain_two, grad_shift_two = norm_pull_two(grad_normed_two)
    grad_residual = upstream + grad_residual_norm
    residual_block_gradient = grad_residual.astype(jnp.bfloat16)
    grad_out_proj = jnp.einsum(
        "azk,azx->kx", attended_block, residual_block_gradient, preferred_element_type=jnp.float32
    )
    grad_attended_b = jnp.einsum(
        "wri,yi->wry",
        residual_block_gradient,
        matrix_out,
        preferred_element_type=jnp.float32,
    ).astype(jnp.bfloat16)
    grad_attended_b, grad_up, down_weight_gradient = lax.optimization_barrier(
        (
            grad_attended_b,
            grad_up.astype(jnp.bfloat16),
            down_weight_gradient.astype(jnp.bfloat16),
        )
    )
    total_up = owner_sum(grad_up, 1, True)
    total_down = owner_sum(down_weight_gradient, 0, False)
    grad_mixed = attend_back(
        mixed,
        lax.all_to_all(grad_attended_b, "seq", split_axis=0, concat_axis=1, tiled=True),
        segment_rows,
        segment_cols,
    )
    mixed_block_gradient = lax.all_to_all(
        jnp.concatenate(grad_mixed, axis=-1), "seq", split_axis=1, concat_axis=0, tiled=True
    )
    mixed_sums = over_tokens(mixed_block_gradient.astype(jnp.float32))
    query_key_value_gradient = jnp.einsum(
        "azk,azx->kx", normalized_block, mixed_block_gradient, preferred_element_type=jnp.float32
    )
    grad_normed = jnp.einsum(
        "wri,yi->wry",
        mixed_block_gradient,
        matrix_qkv,
        preferred_element_type=jnp.float32,
    )
    grad_features, grad_gain_one, grad_shift_one = norm_pull_one(grad_normed)
    input_grad = grad_residual + grad_features
    small_head = jnp.stack(
        [
            grad_gain_one,
            grad_shift_one,
            mixed_sums[:model_width],
            mixed_sums[2 * model_width :],
            over_tokens(grad_residual),
            grad_gain_two,
            grad_shift_two,
            over_tokens(upstream),
        ]
    )
    grad_small = jnp.concatenate(
        [small_head, over_tokens(grad_hidden).reshape(-1, model_width)], axis=0
    )
    grad_mixing = jnp.concatenate([query_key_value_gradient, grad_out_proj], axis=1)
    middle = grad_mixing.shape[1] // 2
    total_rows = jnp.concatenate(
        [
            owner_sum(grad_mixing[:, :middle], 1, True),
            owner_sum(grad_mixing[:, middle:], 1, False),
            total_up,
        ],
        axis=1,
    )
    small_width = smalls.shape[1]
    total_small = lax.dynamic_slice_in_dim(
        lax.psum(grad_small, ("seq", "replica", "fsdp")),
        lax.axis_index("fsdp") * small_width,
        small_width,
        1,
    )
    new_rows, moment_rows, second_rows = adam_update(
        w_rows, m_rows, v_rows, total_rows, rate_rows, weight_decay
    )
    new_down, moment_down, second_down = adam_update(
        w_down, m_down, v_down, total_down, rate_down, weight_decay
    )
    new_small, moment_small, second_small = adam_update(
        smalls, m_small, v_small, total_small, rate_small, 0.0
    )
    return (
        activations,
        input_grad,
        new_rows,
        moment_rows,
        second_rows,
        new_down,
        moment_down,
        second_down,
        new_small,
        moment_small,
        second_small,
    )


def solution(mesh):
    in_specs = (
        P(("fsdp", "replica"), "seq", None),
        P(("fsdp", "replica"), None),
        P(("fsdp", "replica"), "seq", None),
        P("fsdp", None),
        P("fsdp", None),
        P("fsdp", None),
        P("fsdp", None),
        P("fsdp", None),
        P("fsdp", None),
        P(None, "fsdp"),
        P(None, "fsdp"),
        P(None, "fsdp"),
    )
    out_specs = (
        P(("fsdp", "replica"), "seq", None),
        P(("fsdp", "replica"), "seq", None),
        P("fsdp", None),
        P("fsdp", None),
        P("fsdp", None),
        P("fsdp", None),
        P("fsdp", None),
        P("fsdp", None),
        P(None, "fsdp"),
        P(None, "fsdp"),
        P(None, "fsdp"),
    )
    return jax.shard_map(body, mesh=mesh, in_specs=in_specs, out_specs=out_specs, check_vma=False)
```

time: 1120 us -> 833 us (0.74)
  waiting for transfers between devices: 596 us -> 290 us
  matrix products: 266 us -> 93.1 us
  Pallas kernels: 0 us -> 65.4 us
  starting transfers between devices: 0.41 us -> 43.9 us
  other arithmetic: 113 us -> 155 us
  local copies, waits for them, and re-layouts: 95.3 us -> 123 us
    reduce_scatter x4, waiting for transfers between devices: 301 us -> 29 us  [reduce_to_owner(): values = lax.psum_scatter(values, 'fsdp', scatter_dimension=0, tiled=False)]
    dot_general x22 -> x8, matrix products: 232 us -> 63.7 us  [the longest x1 19.2 us: body(): jnp.einsum('tuy,qy->tuq', cotangent, matrix_down, preferred_element_type=...]
    ppermute x0 -> x27, waiting for transfers between devices: none -> 90 us  [partner(): return lax.ppermute(values, axis, [(i, i ^ bit) for i in range(size)])]
    all_gather x4 -> x3, waiting for transfers between devices: 228 us -> 142 us  [gather_columns(): full = lax.all_gather(own, 'fsdp', axis=0, tiled=True)]
    concatenate x0 -> x1, local copies, waits for them, and re-layouts: none -> 67.1 us  [body(): jnp.concatenate(grad_mixed, axis=-1)]
    pallas_call x0 -> x2, Pallas kernels: none -> 65.4 us  [the longest x1 38.7 us: attend_back(): pl.pallas_call(functools.partial(attend_back_kernel, width // H), grid=(c...]
    unnamed x3 -> x7, other arithmetic: 1.25 us -> 61.8 us
    psum x1 -> x0, waiting for transfers between devices: 60.4 us -> none  [body(): lax.psum(shard_rows.astype(jnp.bfloat16), ('seq', 'replica'))]
  transfers between devices with their start and end apart: 10 -> 38, of which waited for: 9 -> 18; matrix products, arithmetic and copies ran while one was open for 18% -> 33% of each run, Pallas kernels for 0% -> 8%
where the time goes in v1:
time: 833 us; the launch traced here: 824 us
  waiting for transfers between devices  290 us (35%)
  other arithmetic  155 us (19%)
  local copies, waits for them, and re-layouts  123 us (15%)
  matrix products  93.1 us (11%)
  Pallas kernels  65.4 us (8%)
  starting transfers between devices  43.9 us (5%)
  blocking collectives  38.6 us (5%)
  between operations  15.6 us (2%)
    all_gather x3, waiting for transfers between devices, gather_columns(): full = lax.all_gather(own, 'fsdp', axis=0, tiled=True)  142 us
    ppermute x27, waiting for transfers between devices, partner(): return lax.ppermute(values, axis, [(i, i ^ bit) for i in range(size)])  90 us
    concatenate x1, local copies, waits for them, and re-layouts, body(): jnp.concatenate(grad_mixed, axis=-1)  67.1 us
    unnamed x7, other arithmetic  61.8 us
    pallas_call x1, Pallas kernels, attend_back(): pl.pallas_call(functools.partial(attend_back_kernel, width // H), grid=(c...  38.7 us
    psum x1, blocking collectives, body(): lax.psum(grad_small, ('seq', 'replica', 'fsdp'))  38.6 us
    unnamed x89, local copies, waits for them, and re-layouts  35 us
    reduce_scatter x4, waiting for transfers between devices, reduce_to_owner(): values = lax.psum_scatter(values, 'fsdp', scatter_dimension=0, tiled=False)  29 us
  transfers between devices with their start and end apart: 38, of which 18 were waited for; matrix products, arithmetic and copies ran while one was open for 33% of the time, Pallas kernels for 8%

profile of v1, /device:TPU:0, one launch (start us, length us, event | category | flops | bytes accessed | tf_op | source)
XLA Modules:
  0.0 824.1 jit_solution(14069256586241014748)
XLA Ops:
  13.2 46.4 %all-gather.4.cloned.1.call-done = bf16[768,1280]{1,0:T(8,128)(2,1)} async-done(((bf16[192,1280]{1,0:T(8,128)(2,1)}), bf16[768,1280]{1,0:T(8,128)(2,1)}) %all-gather.4.cloned.1.call-update) | async-done | bytes 1966096 | tf_op jit(solution)/shard_map/all_gather | solution.py:215
  75.1 5.8 add_convert_fusion
  80.9 5.0 all-to-all-start
  85.9 34.7 %all-gather.8.cloned.1.call-done = bf16[3072,384]{1,0:T(8,128)(2,1)} async-done(((bf16[768,384]{1,0:T(8,128)(2,1)}), bf16[3072,384]{1,0:T(8,128)(2,1)}) %all-gather.8.cloned.1.call-update) | async-done | bytes 2359312 | tf_op jit(solution)/shard_map/all_gather | solution.py:215
  120.6 61.2 %all-gather.6.cloned.1.call-done = bf16[768,1920]{1,0:T(8,128)(2,1)} async-done(((bf16[192,1920]{1,0:T(8,128)(2,1)}), bf16[768,1920]{1,0:T(8,128)(2,1)}) %all-gather.6.cloned.1.call-update) | async-done | bytes 2949136 | tf_op jit(solution)/shard_map/all_gather | solution.py:215
  182.9 26.7 %shard_map.203 = bf16[1,1024,768]{2,1,0:T(8,128)(2,1)S(1)} custom-call(bf16[1,1024,2304]{2,1,0:T(8,128)(2,1)} %bitcast.3.q_ref.k_ref.v_ref, bf16[1,1024,2304]{2,1,0:T(8,128)(2,1)} %bitcast.3.q_ref.k_ref.v_ref, bf16[1,1024,2304]{2,1,0:T(8,128)(2,1)} %bitcast.3.q_ref.k_ref.v_ref, s32[1,1,1024]{2,1,0:T(1,128)S(1)} %get-tuple-element.87.row_ref, ...), custom_call_target="tpu_custom_call" | custom-call | flops 2415919104 | bytes 6291456 | tf_op jit(solution)/shard_map/pallas_call | solution.py:163
  214.2 12.4 %reduce.17 = bf16[1024,768]{1,0:T(8,128)(2,1)} reduce(bf16[1024,1,768]{2,1,0:T(2,128)(2,1)} %bitcast.98, bf16[]{:T(256)} %broadcast.169), dimensions={1}, to_apply=%bitcast.95.reduce_sub_computation | reduce | bytes 3145730
  230.3 4.7 all-to-all-start.1
  235.4 19.8 %all-to-all-done.1 = bf16[4,2,98304]{2,1,0:T(2,128)(2,1)} async-done(((bf16[4,2,98304]{2,1,0:T(2,128)(2,1)}), bf16[4,2,98304]{2,1,0:T(2,128)(2,1)}, u32[]{:S(2)}, u32[]{:S(2)}) %all-to-all-start.1) | async-done | bytes 1572896 | tf_op jit(solution)/shard_map/all_to_all | solution.py:320
  262.2 5.0 broadcast_select_fusion.3
  271.7 8.4 %fusion.32 = f32[4,256,3072]{2,1,0:T(8,128)} fusion(bf16[768,1920]{1,0:T(8,128)(2,1)S(1)} %get-tuple-element.59, bf16[768,1920]{1,0:T(8,128)(2,1)S(1)} %get-tuple-element.60, f32[4,256,768]{2,1,0:T(8,128)S(1)} %get-tuple-element.91, f32[768]{0:T(1024)S(1)} %get-tuple-element.42, f32[768]{0:T(1024)S(1)} %get-tuple-element.40, f32[4,256]{1,0:T(4,128)S(1)} %fusion.45, ...), kind=kOutput, calls=%fused_computation.67 | convolution fusion | flops 4845207552 | bytes 21641216 | tf_op jit(solution)/shard_map/tyr,rw->tyw/dot_general | solution.py:334
  280.1 10.9 %bitcast_convert_fusion = bf16[3072,768]{1,0:T(8,128)(2,1)S(1)} fusion(bf16[4,256,768]{2,1,0:T(8,128)(2,1)S(1)} %copy-done.13, f32[4,256,3072]{2,1,0:T(8,128)} %fusion.32, f32[3072]{0:T(1024)S(1)} %add.283), kind=kOutput, calls=%fused_computation.14 | convolution fusion | flops 4865654784 | bytes 18886656 | tf_op jit(solution)/shard_map/ezg,ezv->gv/dot_general | solution.py:355
  291.0 19.2 %fusion.61 = (f32[3072]{0:T(1024)S(1)}, bf16[4,256,3072]{2,1,0:T(8,128)(2,1)}) fusion(f32[4,256,3072]{2,1,0:T(8,128)} %fusion.32, f32[3072]{0:T(1024)S(1)} %add.283, bf16[4,256,768]{2,1,0:T(8,128)(2,1)S(1)} %copy-done.13, bf16[3072,384]{1,0:T(8,128)(2,1)} %get-tuple-element.63, bf16[3072,384]{1,0:T(8,128)(2,1)} %get-tuple-element.62), kind=kOutput, calls=%fused_computation.178 | convolution fusion | flops 4910478336 | bytes 25190400 | tf_op jit(solution)/shard_map/tuy,qy->tuq/dot_general | solution.py:358
  310.2 8.4 %multiply_reduce_fusion = (f32[768]{0:T(1024)S(1)}, f32[4,256]{1,0:T(4,128)S(1)}, f32[768]{0:T(1024)S(1)}, f32[4,256,768]{2,1,0:T(8,128)S(1)}) fusion(f32[4,256,768]{2,1,0:T(8,128)S(1)} %get-tuple-element.91, f32[4,256]{1,0:T(4,128)S(1)} %fusion.45, f32[4,256]{1,0:T(4,128)S(1)} %broadcast_multiply_fusion, f32[768]{0:T(1024)S(1)} %get-tuple-element.40, ...), kind=kOutput, calls=%fused_computation.53 | convolution fusion | flops 4847563776 | bytes 18502656 | tf_op jit(solution)/shard_map/naz,ez->nae/dot_general | solution.py:369
  318.6 9.9 %bitcast_convert_fusion.1 = bf16[768,3072]{1,0:T(8,128)(2,1)} fusion(bf16[4,256,3072]{2,1,0:T(8,128)(2,1)} %get-tuple-element.95, f32[4,256,768]{2,1,0:T(8,128)S(1)} %get-tuple-element.91, f32[768]{0:T(1024)S(1)} %get-tuple-element.42, f32[768]{0:T(1024)S(1)} %get-tuple-element.40, f32[4,256]{1,0:T(4,128)S(1)} %fusion.45, ...), kind=kOutput, calls=%fused_computation.15 | convolution fusion | flops 4838129664 | bytes 14170112 | tf_op jit(solution)/shard_map/zng,znw->gw/dot_general | solution.py:363
  356.2 8.5 %all-to-all-done.2 = bf16[4,256,768]{2,1,0:T(8,128)(2,1)} async-done(((bf16[4,256,768]{2,1,0:T(8,128)(2,1)}), bf16[4,256,768]{2,1,0:T(8,128)(2,1)}, u32[]{:S(2)}, u32[]{:S(2)}) %all-to-all-start.2) | async-done | bytes 1572896 | tf_op jit(solution)/shard_map/all_to_all | solution.py:398
  364.7 38.7 %shard_map.204 = (bf16[1,1024,768]{2,1,0:T(8,128)(2,1)S(1)}, bf16[1,1024,768]{2,1,0:T(8,128)(2,1)S(1)}, bf16[1,1024,768]{2,1,0:T(8,128)(2,1)S(1)}) custom-call(bf16[1,1024,2304]{2,1,0:T(8,128)(2,1)} %bitcast.3.q_ref.k_ref.v_ref, bf16[1,1024,2304]{2,1,0:T(8,128)(2,1)} %bitcast.3.q_ref.k_ref.v_ref, bf16[1,1024,2304]{2,1,0:T(8,128)(2,1)} %bitcast.3.q_ref.k_ref.v_ref, ...), custom_call_target="tpu_custom_call" | custom-call | flops 5637144576 | bytes 11010048 | tf_op jit(solution)/shard_map/pallas_call | solution.py:183
  403.8 67.1 %copy.70 = bf16[1,1024,2304]{2,0,1:T(2,128)(2,1)} copy(bf16[1,1024,2304]{2,1,0:T(8,128)(2,1)S(1)} %pad_maximum_fusion.1) | data formatting | bytes 9437184 | tf_op jit(solution)/shard_map/concatenate | solution.py:403
  470.8 49.0 %reduce.18 = bf16[1024,2304]{1,0:T(8,128)(2,1)} reduce(bf16[1024,1,2304]{2,1,0:T(2,128)(2,1)} %bitcast.97, bf16[]{:T(256)} %broadcast.169), dimensions={1}, to_apply=%bitcast.94.reduce_sub_computation | reduce | bytes 9437186
  519.8 5.4 reshape.144
  525.2 4.9 all-to-all-start.3
  539.4 57.2 %collective-permute-done.23 = bf16[4,96,768]{2,1,0:T(8,128)(2,1)} collective-permute-done((bf16[4,96,768]{2,1,0:T(8,128)(2,1)S(1)}, bf16[4,96,768]{2,1,0:T(8,128)(2,1)}, u32[]{:S(2)}, u32[]{:S(2)}) %collective-permute-start.23) | collective-permute-done | bytes 589856 | tf_op jit(solution)/shard_map/ppermute | solution.py:201
  598.8 13.6 %add_convert_fusion.3 = bf16[4,256,768]{2,1,0:T(8,128)(2,1)} fusion(f32[4,256,768]{2,1,0:T(8,128)} %copy-done.4, f32[768]{0:T(1024)S(1)} %get-tuple-element.41, bf16[3072,384]{1,0:T(8,128)(2,1)} %get-tuple-element.63, bf16[3072,384]{1,0:T(8,128)(2,1)} %get-tuple-element.62, f32[4,256,3072]{2,1,0:T(8,128)} %fusion.32, f32[3072]{0:T(1024)S(1)} %add.283), kind=kOutput, calls=%fused_computation.59 | convolution fusion | flops 4875091968 | bytes 22035456 | tf_op jit(solution)/shard_map/crx,xo->cro/dot_general | solution.py:345
  618.6 8.4 %reshape.145 = bf16[1024,1,2304]{2,1,0:T(2,128)(2,1)} reshape(bf16[4,2,294912]{2,1,0:T(2,128)(2,1)} %all-to-all-done.3) | data formatting | bytes 9437184
  626.9 20.8 %convert_reduce_fusion = f32[2304]{0:T(1024)S(1)} fusion(bf16[1024,1,2304]{2,1,0:T(2,128)(2,1)} %reshape.145), kind=kLoop, calls=%fused_computation.16 | loop fusion | flops 4716288 | bytes 4727808 | tf_op jit(solution)/shard_map/reduce_sum | solution.py:286
  667.5 38.6 %psum.7 = f32[12,768]{1,0:T(8,128)S(1)} all-reduce(f32[12,768]{1,0:T(8,128)S(1)} %concatenate.80), channel_id=1, replica_groups=mesh['seq'=4,'fsdp'=4,'replica'=2] {'seq','replica','fsdp'}, use_global_device_ids=true, to_apply=%region_20.21 | all-reduce | flops 9216 | bytes 73728 | tf_op jit(solution)/shard_map/psum | solution.py:444
  727.6 11.6 %collective-permute-done.4 = bf16[4,192,384]{2,1,0:T(8,128)(2,1)S(1)} collective-permute-done((bf16[4,192,384]{2,1,0:T(8,128)(2,1)S(1)}, bf16[4,192,384]{2,1,0:T(8,128)(2,1)S(1)}, u32[]{:S(2)}, u32[]{:S(2)}) %collective-permute-start.4) | collective-permute-done | bytes 589856 | tf_op jit(solution)/shard_map/ppermute | solution.py:201
  743.8 6.5 collective-permute-done.5
  755.3 15.9 %reduce-scatter.5.cloned.1.call-done = bf16[1,192,192]{2,1,0:T(8,128)(2,1)} async-done(((bf16[4,192,192]{2,1,0:T(8,128)(2,1)}), bf16[1,192,192]{2,1,0:T(8,128)(2,1)}) %reduce-scatter.5.cloned.1.call-update) | async-done | bytes 73744 | tf_op jit(solution)/shard_map/reduce_scatter | solution.py:247
  772.7 7.4 multiply_subtract_fusion.1
  780.1 13.0 %reduce-scatter.7.cloned.1.call-done = bf16[1,192,192]{2,1,0:T(8,128)(2,1)} async-done(((bf16[4,192,192]{2,1,0:T(8,128)(2,1)}), bf16[1,192,192]{2,1,0:T(8,128)(2,1)}) %reduce-scatter.7.cloned.1.call-update) | async-done | bytes 73744 | tf_op jit(solution)/shard_map/reduce_scatter | solution.py:247
  806.8 10.1 %multiply_subtract_fusion = (f32[192,6144]{1,0:T(8,128)}, f32[192,6144]{1,0:T(8,128)}, f32[192,6144]{1,0:T(8,128)}) fusion(f32[192,6144]{1,0:T(8,128)} %param.15, bf16[192,6144]{1,0:T(8,128)(2,1)S(1)} %select_dynamic-update-slice_fusion, f32[192,6144]{1,0:T(8,128)} %param.16, f32[192,6144]{1,0:T(8,128)} %param.17), kind=kLoop, calls=%fused_computation.37 | loop fusion | flops 18874368 | bytes 30670848 | tf_op jit(solution)/shard_map/sub | solution.py:40
  (265 shorter events, 153.3 us)
Async XLA Ops:
  7.2 52.3 %all-gather.4.cloned.1.call-start = ((), (), s32[]{:S(2)}) async-start(), calls=%async_computation.8 | async-start | bytes 2457600 | tf_op jit(solution)/shard_map/all_gather | solution.py:215
  13.1 107.5 %all-gather.8.cloned.1.call-start = ((), (), s32[]{:S(2)}) async-start(), calls=%async_computation.10 | async-start | bytes 2949120 | tf_op jit(solution)/shard_map/all_gather | solution.py:215
  71.2 110.7 %all-gather.6.cloned.1.call-start = ((), (), s32[]{:S(2)}) async-start(), calls=%async_computation.9 | async-start | bytes 3686400 | tf_op jit(solution)/shard_map/all_gather | solution.py:215
  80.9 101.9 %all-to-all-start = ((bf16[4,256,2304]{2,1,0:T(8,128)(2,1)}), bf16[4,256,2304]{2,1,0:T(8,128)(2,1)}, u32[]{:S(2)}, u32[]{:S(2)}) async-start(bf16[4,256,2304]{2,1,0:T(8,128)(2,1)} %add_convert_fusion), calls=%async_computation | async-start | bytes 9437184 | tf_op jit(solution)/shard_map/all_to_all | solution.py:311
  120.6 141.3 %collective-permute-start.2 = (bf16[3072,384]{1,0:T(8,128)(2,1)}, bf16[3072,384]{1,0:T(8,128)(2,1)}, u32[]{:S(2)}, u32[]{:S(2)}) collective-permute-start(bf16[3072,384]{1,0:T(8,128)(2,1)} %all-gather.8.cloned.1.call-done), channel_id=1, source_target_pairs={{0,8},{8,0},{16,24},{24,16},{1,9},{9,1},{17,25},{25,17},{2,10},{10... | collective-permute-start | bytes 7077896 | tf_op jit(solution)/shard_map/ppermute | solution.py:201
  181.9 85.3 %collective-permute-start.1 = (bf16[768,1920]{1,0:T(8,128)(2,1)}, bf16[768,1920]{1,0:T(8,128)(2,1)}, u32[]{:S(2)}, u32[]{:S(2)}) collective-permute-start(bf16[768,1920]{1,0:T(8,128)(2,1)} %all-gather.6.cloned.1.call-done), channel_id=1, source_target_pairs={{0,8},{8,0},{16,24},{24,16},{1,9},{9,1},{17,25},{25,17},{2,10},{10... | collective-permute-start | bytes 8847368 | tf_op jit(solution)/shard_map/ppermute | solution.py:201
  230.3 24.9 %all-to-all-start.1 = ((bf16[4,2,98304]{2,1,0:T(2,128)(2,1)}), bf16[4,2,98304]{2,1,0:T(2,128)(2,1)}, u32[]{:S(2)}, u32[]{:S(2)}) async-start(bf16[4,2,98304]{2,1,0:T(2,128)(2,1)} %reshape.142), calls=%async_computation.1 | async-start | bytes 3145728 | tf_op jit(solution)/shard_map/all_to_all | solution.py:320
  336.0 8.1 collective-permute-start.21
  339.3 9.5 %collective-permute-start.15 = (bf16[4,192,1536]{2,1,0:T(8,128)(2,1)}, bf16[4,192,1536]{2,1,0:T(8,128)(2,1)}, u32[]{:S(2)}, u32[]{:S(2)}) collective-permute-start(bf16[4,192,1536]{2,1,0:T(8,128)(2,1)} %constant_dynamic-slice_fusion.5), channel_id=1, source_target_pairs={{0,8},{8,0},{16,24},{24,16},{1,9},{9,1},{17,25},{25,17},{2,10},{10... | collective-permute-start | bytes 7077896 | tf_op jit(solution)/shard_map/ppermute | solution.py:201
  339.8 25.0 %all-to-all-start.2 = ((bf16[4,256,768]{2,1,0:T(8,128)(2,1)}), bf16[4,256,768]{2,1,0:T(8,128)(2,1)}, u32[]{:S(2)}, u32[]{:S(2)}) async-start(bf16[4,256,768]{2,1,0:T(8,128)(2,1)} %convolution_convert_fusion), calls=%async_computation.2 | async-start | bytes 3145728 | tf_op jit(solution)/shard_map/all_to_all | solution.py:398
  347.2 183.0 %collective-permute-start.22 = (bf16[4,192,768]{2,1,0:T(8,128)(2,1)S(1)}, bf16[4,192,768]{2,1,0:T(8,128)(2,1)}, u32[]{:S(2)}, u32[]{:S(2)}) collective-permute-start(bf16[4,192,768]{2,1,0:T(8,128)(2,1)S(1)} %constant_dynamic-slice_fusion.1), channel_id=1, source_target_pairs={{0,1},{1,0},{2,3},{3,2},{4,5},{5,4},{6,7},{7,6},{8,9},{9,8},{10,11... | collective-permute-start | bytes 3538952 | tf_op jit(solution)/shard_map/ppermute | solution.py:201
  354.3 179.9 %collective-permute-start.16 = (bf16[4,192,768]{2,1,0:T(8,128)(2,1)}, bf16[4,192,768]{2,1,0:T(8,128)(2,1)}, u32[]{:S(2)}, u32[]{:S(2)}) collective-permute-start(bf16[4,192,768]{2,1,0:T(8,128)(2,1)} %constant_dynamic-slice_fusion.4), channel_id=1, source_target_pairs={{0,16},{8,24},{16,0},{24,8},{1,17},{9,25},{17,1},{25,9},{2,18},{10... | collective-permute-start | bytes 3538952 | tf_op jit(solution)/shard_map/ppermute | solution.py:201
  525.2 93.3 %all-to-all-start.3 = ((bf16[4,2,294912]{2,1,0:T(2,128)(2,1)}), bf16[4,2,294912]{2,1,0:T(2,128)(2,1)}, u32[]{:S(2)}, u32[]{:S(2)}) async-start(bf16[4,2,294912]{2,1,0:T(2,128)(2,1)} %reshape.144), calls=%async_computation.3 | async-start | bytes 9437184 | tf_op jit(solution)/shard_map/all_to_all | solution.py:402
  530.1 175.9 %reduce-scatter.11.cloned.1.call-start = ((), (), s32[]{:S(2)}) async-start(), calls=%async_computation.14 | async-start | bytes 737280 | tf_op jit(solution)/shard_map/reduce_scatter | solution.py:247
  532.2 64.5 %collective-permute-start.23 = (bf16[4,96,768]{2,1,0:T(8,128)(2,1)S(1)}, bf16[4,96,768]{2,1,0:T(8,128)(2,1)}, u32[]{:S(2)}, u32[]{:S(2)}) collective-permute-start(bf16[4,96,768]{2,1,0:T(8,128)(2,1)S(1)} %constant_dynamic-slice_fusion), channel_id=1, source_target_pairs={{0,16},{8,24},{16,0},{24,8},{1,17},{9,25},{17,1},{25,9},{2,18},{10... | collective-permute-start | bytes 1769480 | tf_op jit(solution)/shard_map/ppermute | solution.py:201
  538.0 78.5 %collective-permute-start.17 = (bf16[4,192,384]{2,1,0:T(8,128)(2,1)}, bf16[4,192,384]{2,1,0:T(8,128)(2,1)}, u32[]{:S(2)}, u32[]{:S(2)}) collective-permute-start(bf16[4,192,384]{2,1,0:T(8,128)(2,1)} %constant_dynamic-slice_fusion.3), channel_id=1, source_target_pairs={{0,1},{1,0},{2,3},{3,2},{4,5},{5,4},{6,7},{7,6},{8,9},{9,8},{10,11... | collective-permute-start | bytes 1769480 | tf_op jit(solution)/shard_map/ppermute | solution.py:201
  598.7 110.5 %reduce-scatter.9.cloned.1.call-start = ((), (), s32[]{:S(2)}) async-start(), calls=%async_computation.13 | async-start | bytes 737280 | tf_op jit(solution)/shard_map/reduce_scatter | solution.py:247
  618.5 152.7 %reduce-scatter.5.cloned.1.call-start = ((), (), s32[]{:S(2)}) async-start(), calls=%async_computation.11 | async-start | bytes 491520 | tf_op jit(solution)/shard_map/reduce_scatter | solution.py:247
  665.6 58.7 %collective-permute-start.9 = (bf16[4,192,768]{2,1,0:T(8,128)(2,1)S(1)}, bf16[4,192,768]{2,1,0:T(8,128)(2,1)}, u32[]{:S(2)}, u32[]{:S(2)}) collective-permute-start(bf16[4,192,768]{2,1,0:T(8,128)(2,1)S(1)} %constant_dynamic-slice_fusion.8), channel_id=1, source_target_pairs={{0,8},{8,0},{16,24},{24,16},{1,9},{9,1},{17,25},{25,17},{2,10},{10... | collective-permute-start | bytes 3538952 | tf_op jit(solution)/shard_map/ppermute | solution.py:201
  667.4 54.4 %collective-permute-start.3 = (bf16[4,192,768]{2,1,0:T(8,128)(2,1)}, bf16[4,192,768]{2,1,0:T(8,128)(2,1)}, u32[]{:S(2)}, u32[]{:S(2)}) collective-permute-start(bf16[4,192,768]{2,1,0:T(8,128)(2,1)} %constant_dynamic-slice_fusion.11), channel_id=1, source_target_pairs={{0,8},{8,0},{16,24},{24,16},{1,9},{9,1},{17,25},{25,17},{2,10},{10... | collective-permute-start | bytes 3538952 | tf_op jit(solution)/shard_map/ppermute | solution.py:201
  709.2 6.3 collective-permute-start.18
  712.7 8.1 collective-permute-start.25
  716.5 11.0 %collective-permute-start.19 = (bf16[192,768]{1,0:T(8,128)(2,1)S(1)}, bf16[192,768]{1,0:T(8,128)(2,1)S(1)}, u32[]{:S(2)}, u32[]{:S(2)}) collective-permute-start(bf16[192,768]{1,0:T(8,128)(2,1)S(1)} %pad_maximum_fusion.9), channel_id=1, source_target_pairs={{0,16},{8,24},{16,0},{24,8},{1,17},{9,25},{17,1},{25,9},{2,18},{10... | collective-permute-start | bytes 884744 | tf_op jit(solution)/shard_map/ppermute | solution.py:201
  721.8 30.4 %collective-permute-start.26 = (bf16[384,768]{1,0:T(8,128)(2,1)}, bf16[384,768]{1,0:T(8,128)(2,1)}, u32[]{:S(2)}, u32[]{:S(2)}) collective-permute-start(bf16[384,768]{1,0:T(8,128)(2,1)} %pad_maximum_fusion.6), channel_id=1, source_target_pairs={{0,8},{8,0},{16,24},{24,16},{1,9},{9,1},{17,25},{25,17},{2,10},{10... | collective-permute-start | bytes 1769480 | tf_op jit(solution)/shard_map/ppermute | solution.py:201
  723.5 15.7 %collective-permute-start.4 = (bf16[4,192,384]{2,1,0:T(8,128)(2,1)S(1)}, bf16[4,192,384]{2,1,0:T(8,128)(2,1)S(1)}, u32[]{:S(2)}, u32[]{:S(2)}) collective-permute-start(bf16[4,192,384]{2,1,0:T(8,128)(2,1)S(1)} %constant_dynamic-slice_fusion.10), channel_id=1, source_target_pairs={{0,16},{8,24},{16,0},{24,8},{1,17},{9,25},{17,1},{25,9},{2,18},{10... | collective-permute-start | bytes 1769480 | tf_op jit(solution)/shard_map/ppermute | solution.py:201
  726.0 15.4 %collective-permute-start.10 = (bf16[4,192,384]{2,1,0:T(8,128)(2,1)S(1)}, bf16[4,192,384]{2,1,0:T(8,128)(2,1)S(1)}, u32[]{:S(2)}, u32[]{:S(2)}) collective-permute-start(bf16[4,192,384]{2,1,0:T(8,128)(2,1)S(1)} %constant_dynamic-slice_fusion.7), channel_id=1, source_target_pairs={{0,1},{1,0},{2,3},{3,2},{4,5},{5,4},{6,7},{7,6},{8,9},{9,8},{10,11... | collective-permute-start | bytes 1769480 | tf_op jit(solution)/shard_map/ppermute | solution.py:201
  739.6 10.7 %collective-permute-start.5 = (bf16[4,192,192]{2,1,0:T(8,128)(2,1)S(1)}, bf16[4,192,192]{2,1,0:T(8,128)(2,1)S(1)}, u32[]{:S(2)}, u32[]{:S(2)}) collective-permute-start(bf16[4,192,192]{2,1,0:T(8,128)(2,1)S(1)} %constant_dynamic-slice_fusion.9), channel_id=1, source_target_pairs={{0,1},{1,0},{2,3},{3,2},{4,5},{5,4},{6,7},{7,6},{8,9},{9,8},{10,11... | collective-permute-start | bytes 884744 | tf_op jit(solution)/shard_map/ppermute | solution.py:201
  742.6 11.7 %collective-permute-start.11 = (bf16[4,192,192]{2,1,0:T(8,128)(2,1)}, bf16[4,192,192]{2,1,0:T(8,128)(2,1)S(1)}, u32[]{:S(2)}, u32[]{:S(2)}) collective-permute-start(bf16[4,192,192]{2,1,0:T(8,128)(2,1)} %constant_dynamic-slice_fusion.6), channel_id=1, source_target_pairs={{0,16},{8,24},{16,0},{24,8},{1,17},{9,25},{17,1},{25,9},{2,18},{10... | collective-permute-start | bytes 884744 | tf_op jit(solution)/shard_map/ppermute | solution.py:201
  751.3 41.8 %reduce-scatter.7.cloned.1.call-start = ((), (), s32[]{:S(2)}) async-start(), calls=%async_computation.12 | async-start | bytes 491520 | tf_op jit(solution)/shard_map/reduce_scatter | solution.py:247
  752.2 54.3 %collective-permute-start.20 = (bf16[192,1536]{1,0:T(8,128)(2,1)}, bf16[192,1536]{1,0:T(8,128)(2,1)S(1)}, u32[]{:S(2)}, u32[]{:S(2)}) collective-permute-start(bf16[192,1536]{1,0:T(8,128)(2,1)} %pad_maximum_fusion.5), channel_id=1, source_target_pairs={{0,8},{8,0},{16,24},{24,16},{1,9},{9,1},{17,25},{25,17},{2,10},{10... | collective-permute-start | bytes 1769480 | tf_op jit(solution)/shard_map/ppermute | solution.py:201
  771.2 23.3 %collective-permute-start.6 = (bf16[192,192]{1,0:T(8,128)(2,1)}, bf16[192,192]{1,0:T(8,128)(2,1)S(1)}, u32[]{:S(2)}, u32[]{:S(2)}) collective-permute-start(bf16[192,192]{1,0:T(8,128)(2,1)} %bitcast.115), channel_id=1, source_target_pairs={{0,1},{1,0},{2,3},{3,2},{4,5},{5,4},{6,7},{7,6},{8,9},{9,8},{10,11... | collective-permute-start | bytes 221192 | tf_op jit(solution)/shard_map/ppermute | solution.py:201
  794.7 6.1 collective-permute-start.7
  (49 other events, 446.2 us)
Sparse Core Ops, SparseCore 0:
  13.2 46.2 all-gather.3
  71.3 49.3 all-gather.7
  122.8 59.0 all-gather.5
  598.8 19.7 reduce-scatter.10
  621.3 20.3 reduce-scatter.8
  751.4 19.7 reduce-scatter.4
  774.2 18.8 reduce-scatter.6

commit v2 on v1

--- a/solution.py
+++ b/solution.py
@@ -206,20 +206,41 @@
     return lax.dynamic_slice_in_dim(values, upper * half, half, dim)
 
 
-def gather_columns(values, extra=None):
-    upper = lax.axis_index("seq") & 1
-    own = half_of(values, upper, 1)
-    width = own.shape[1]
-    if extra is not None:
-        own = jnp.concatenate([own, extra], axis=1)
-    full = lax.all_gather(own, "fsdp", axis=0, tiled=True)
-    mine = full[:, :width]
+def gather_half(values):
+    return lax.all_gather(
+        half_of(values, lax.axis_index("seq") & 1, 1), "fsdp", axis=0, tiled=True
+    )
+
+
+def swap_halves(mine):
     other = partner(mine, "seq", 1)
-    first = upper == 0
-    whole = jnp.concatenate(
+    first = lax.axis_index("seq") & 1 == 0
+    return jnp.concatenate(
         [jnp.where(first, mine, other), jnp.where(first, other, mine)], axis=1
     )
-    return whole, full[:, width:]
+
+
+def to_sequences(values):
+    size = lax.axis_size("seq")
+    count, piece, width = values.shape
+    values = lax.all_to_all(values, "seq", split_axis=0, concat_axis=0, tiled=True)
+    values = jnp.moveaxis(values.reshape(size, count // size, piece, width), 0, 1)
+    return values.reshape(count // size, size * piece, width)
+
+
+def to_pieces(values):
+    size = lax.axis_size("seq")
+    count, length, width = values.shape
+    values = jnp.moveaxis(values.reshape(count, size, length // size, width), 1, 0)
+    values = values.reshape(size * count, length // size, width)
+    return lax.all_to_all(values, "seq", split_axis=0, concat_axis=0, tiled=True)
+
+
+def butterfly_sum(values, axes):
+    for axis in axes:
+        for bit in range(lax.axis_size(axis).bit_length() - 1):
+            values = values + partner(values, axis, 1 << bit)
+    return values
 
 
 def halve(values, axis, bit, dim):
@@ -235,17 +256,20 @@
     return seq_bits[:1], seq_bits[1:], replica_bits
 
 
-def reduce_to_owner(values, dim, seq_first):
+def by_owner(values):
     shards = lax.axis_size("fsdp")
     values = values.astype(jnp.bfloat16)
-    values = values.reshape((shards, values.shape[0] // shards) + values.shape[1:])
-    cut = 2 if dim == 1 else 1
-    first, rest, replicas = plane_steps()
-    steps = first + (rest + replicas if seq_first else replicas + rest)
+    return values.reshape((shards, values.shape[0] // shards) + values.shape[1:])
+
+
+def halve_all(values, steps, cut):
     for axis, bit in steps:
         values = halve(values, axis, bit, cut)
-    values = lax.psum_scatter(values, "fsdp", scatter_dimension=0, tiled=False)
-    return values, steps
+    return values
+
+
+def scatter_rows(values):
+    return lax.psum_scatter(values, "fsdp", scatter_dimension=0, tiled=False)
 
 
 def collect(values, steps, dim):
@@ -257,11 +281,6 @@
             [jnp.where(first, values, other), jnp.where(first, other, values)], axis=dim
         )
     return values
-
-
-def owner_sum(values, dim, seq_first):
-    part, steps = reduce_to_owner(values, dim, seq_first)
-    return collect(part, steps, dim).astype(jnp.float32)
 
 
 def body(
@@ -287,19 +306,18 @@
 
     rows_b = w_rows.astype(jnp.bfloat16)
     small_pad = jnp.pad(smalls.astype(jnp.bfloat16).T, ((0, 0), (0, LANES - small_rows)))
-    matrix_qkv, small_full = gather_columns(rows_b[:, :query_key_value_boundary], small_pad)
-    rows_rest, down_b, matrix_qkv, small_full = lax.optimization_barrier(
-        (
-            rows_b[:, query_key_value_boundary:],
-            w_down.astype(jnp.bfloat16),
-            matrix_qkv,
-            small_full,
-        )
-    )
-    matrix_rest, _ = gather_columns(rows_rest)
-    matrix_down, _ = gather_columns(down_b)
-    matrix_out = matrix_rest[:, :model_width]
-    matrix_up = matrix_rest[:, model_width:]
+    own_qkv = half_of(rows_b[:, :query_key_value_boundary], lax.axis_index("seq") & 1, 1)
+    half_width = own_qkv.shape[1]
+    full_qkv = lax.all_gather(
+        jnp.concatenate([own_qkv, small_pad], axis=1), "fsdp", axis=0, tiled=True
+    )
+    rows_rest, down_b, full_qkv = lax.optimization_barrier(
+        (rows_b[:, query_key_value_boundary:], w_down.astype(jnp.bfloat16), full_qkv)
+    )
+    half_rest = gather_half(rows_rest)
+    half_down = gather_half(down_b)
+    matrix_qkv = swap_halves(full_qkv[:, :half_width])
+    small_full = full_qkv[:, half_width:]
     small_vals = small_full[:, :small_rows].T.astype(jnp.float32)
     features = inputs.astype(jnp.float32)
     normed, norm_pull_one = jax.vjp(normalize, features, small_vals[0], small_vals[1])
@@ -308,18 +326,21 @@
         "rxj,jw->rxw", normalized_block, matrix_qkv, preferred_element_type=jnp.float32
     )
     bias = jnp.concatenate([small_vals[2], jnp.zeros_like(small_vals[2]), small_vals[3]])
-    mixed = lax.all_to_all(
-        (projected + bias).astype(jnp.bfloat16), "seq", split_axis=0, concat_axis=1, tiled=True
-    )
+    mixed = to_sequences((projected + bias).astype(jnp.bfloat16))
     own_count = mixed.shape[0]
     own_segments = lax.dynamic_slice_in_dim(
         segments, lax.axis_index("seq") * own_count, own_count, 0
     )
     segment_rows = own_segments[:, None, :]
     segment_cols = own_segments[:, :, None]
-    attended_block = lax.all_to_all(
-        attend(mixed, segment_rows, segment_cols), "seq", split_axis=1, concat_axis=0, tiled=True
-    )
+    attended_own, half_rest, half_down = lax.optimization_barrier(
+        (attend(mixed, segment_rows, segment_cols), half_rest, half_down)
+    )
+    attended_block = to_pieces(attended_own)
+    matrix_rest = swap_halves(half_rest)
+    matrix_down = swap_halves(half_down)
+    matrix_out = matrix_rest[:, :model_width]
+    matrix_up = matrix_rest[:, model_width:]
     residual = features + (
         jnp.einsum(
             "rxj,jw->rxw",
@@ -391,17 +412,29 @@
             down_weight_gradient.astype(jnp.bfloat16),
         )
     )
-    total_up = owner_sum(grad_up, 1, True)
-    total_down = owner_sum(down_weight_gradient, 0, False)
-    grad_mixed = attend_back(
-        mixed,
-        lax.all_to_all(grad_attended_b, "seq", split_axis=0, concat_axis=1, tiled=True),
-        segment_rows,
-        segment_cols,
-    )
-    mixed_block_gradient = lax.all_to_all(
-        jnp.concatenate(grad_mixed, axis=-1), "seq", split_axis=1, concat_axis=0, tiled=True
-    )
+    first, rest, replicas = plane_steps()
+    part_up = halve_all(by_owner(grad_up), first, 2)
+    part_down = halve_all(by_owner(down_weight_gradient), first, 1)
+    grad_attended_own, part_up, part_down = lax.optimization_barrier(
+        (to_sequences(grad_attended_b), part_up, part_down)
+    )
+    part_up = halve_all(part_up, rest + replicas, 2)
+    part_down = halve_all(part_down, replicas + rest, 1)
+    up_columns = part_up.shape[2]
+    part_down = jnp.concatenate(
+        [part_down[:, :, :up_columns], part_down[:, :, up_columns:]], axis=1
+    )
+    owned = scatter_rows(jnp.concatenate([part_up, part_down], axis=2))
+    total_up = collect(owned[:, :up_columns], first + rest + replicas, 1)
+    owned_down = owned[:, up_columns:]
+    down_rows = owned_down.shape[0] // 2
+    total_down = collect(
+        jnp.concatenate([owned_down[:down_rows], owned_down[down_rows:]], axis=1),
+        first + replicas + rest,
+        0,
+    ).astype(jnp.float32)
+    grad_mixed = attend_back(mixed, grad_attended_own, segment_rows, segment_cols)
+    mixed_block_gradient = to_pieces(jnp.concatenate(grad_mixed, axis=-1))
     mixed_sums = over_tokens(mixed_block_gradient.astype(jnp.float32))
     query_key_value_gradient = jnp.einsum(
         "azk,azx->kx", normalized_block, mixed_block_gradient, preferred_element_type=jnp.float32
@@ -431,17 +464,21 @@
     )
     grad_mixing = jnp.concatenate([query_key_value_gradient, grad_out_proj], axis=1)
     middle = grad_mixing.shape[1] // 2
+    part_left = halve_all(by_owner(grad_mixing[:, :middle]), first + rest + replicas, 2)
+    part_right = halve_all(by_owner(grad_mixing[:, middle:]), first + replicas + rest, 2)
+    left_columns = part_left.shape[2]
+    owned = scatter_rows(jnp.concatenate([part_left, part_right], axis=2))
     total_rows = jnp.concatenate(
         [
-            owner_sum(grad_mixing[:, :middle], 1, True),
-            owner_sum(grad_mixing[:, middle:], 1, False),
+            collect(owned[:, :left_columns], first + rest + replicas, 1),
+            collect(owned[:, left_columns:], first + replicas + rest, 1),
             total_up,
         ],
         axis=1,
-    )
+    ).astype(jnp.float32)
     small_width = smalls.shape[1]
     total_small = lax.dynamic_slice_in_dim(
-        lax.psum(grad_small, ("seq", "replica", "fsdp")),
+        butterfly_sum(grad_small, ("seq", "replica", "fsdp")),
         lax.axis_index("fsdp") * small_width,
         small_width,
         1,

time: 833 us -> 595 us (0.71)
  local copies, waits for them, and re-layouts: 123 us -> 29 us
  other arithmetic: 155 us -> 74.8 us
  blocking collectives: 38.6 us -> 0 us
  waiting for transfers between devices: 290 us -> 256 us
    all_gather x3, waiting for transfers between devices: 142 us -> 53 us  [the longest x1 44.6 us: body(): lax.all_gather(jnp.concatenate([own_qkv, small_pad], axis=1), 'fsdp', axi...]
    concatenate x1 -> x0, local copies, waits for them, and re-layouts: 67.1 us -> none  [body(): jnp.concatenate(grad_mixed, axis=-1)]
    unnamed x7 -> x6, other arithmetic: 61.8 us -> 0.43 us
    all_to_all x4, waiting for transfers between devices: 28.3 us -> 74.2 us  [the longest x2 64.2 us: to_sequences(): lax.all_to_all(values, 'seq', split_axis=0, concat_axis=0, tiled=True)]
    psum x1 -> x0, blocking collectives: 38.6 us -> none  [body(): lax.psum(grad_small, ('seq', 'replica', 'fsdp'))]
    unnamed x89 -> x68, local copies, waits for them, and re-layouts: 35 us -> 7.65 us
    ppermute x27 -> x32, waiting for transfers between devices: 90 us -> 116 us  [partner(): return lax.ppermute(values, axis, [(i, i ^ bit) for i in range(size)])]
    reduce_sum x2, other arithmetic: 23.7 us -> 5.87 us  [over_tokens(): return jnp.sum(values, axis=(0, 1))]
  transfers between devices with their start and end apart: 38 -> 41, of which waited for: 18 -> 22; matrix products, arithmetic and copies ran while one was open for 33% -> 19% of each run, Pallas kernels for 8% -> 5%
where the time goes in v2:
time: 595 us; the launch traced here: 587 us
  waiting for transfers between devices  256 us (43%)
  matrix products  101 us (17%)
  other arithmetic  74.8 us (13%)
  Pallas kernels  65.7 us (11%)
  starting transfers between devices  44.7 us (8%)
  local copies, waits for them, and re-layouts  29 us (5%)
  between operations  15.2 us (3%)
    ppermute x32, waiting for transfers between devices, partner(): return lax.ppermute(values, axis, [(i, i ^ bit) for i in range(size)])  116 us
    all_to_all x2, waiting for transfers between devices, to_sequences(): lax.all_to_all(values, 'seq', split_axis=0, concat_axis=0, tiled=True)  64.2 us
    all_gather x1, waiting for transfers between devices, body(): lax.all_gather(jnp.concatenate([own_qkv, small_pad], axis=1), 'fsdp', axi...  44.6 us
    pallas_call x1, Pallas kernels, attend_back(): pl.pallas_call(functools.partial(attend_back_kernel, width // H), grid=(c...  38.7 us
    pallas_call x1, Pallas kernels, attend(): pl.pallas_call(functools.partial(attend_kernel, width // H), grid=(count,...  27.1 us
    ppermute x32, starting transfers between devices, partner(): return lax.ppermute(values, axis, [(i, i ^ bit) for i in range(size)])  25.2 us
    convert_element_type x12, other arithmetic, halve(): (kept.astype(jnp.float32) + got.astype(jnp.float32)).astype(jnp.bfloat16)  19.2 us
    dot_general x1, matrix products, body(): jnp.einsum('tuy,qy->tuq', cotangent, matrix_down, preferred_element_type=...  18.8 us
  transfers between devices with their start and end apart: 41, of which 22 were waited for; matrix products, arithmetic and copies ran while one was open for 19% of the time, Pallas kernels for 5%

profile of v2, /device:TPU:0, one launch (start us, length us, event | category | flops | bytes accessed | tf_op | source)
XLA Modules:
  0.0 586.6 jit_solution(9806455746605775441)
XLA Ops:
  15.0 44.6 %all-gather.4.cloned.1.call-done = bf16[768,1280]{1,0:T(8,128)(2,1)} async-done(((bf16[192,1280]{1,0:T(8,128)(2,1)}), bf16[768,1280]{1,0:T(8,128)(2,1)}) %all-gather.4.cloned.1.call-update) | async-done | bytes 1966096 | tf_op jit(solution)/shard_map/all_gather | solution.py:311
  72.3 5.8 add_convert_fusion
  78.0 4.9 all-to-all-start
  83.9 52.9 %all-to-all-done = bf16[4,256,2304]{2,1,0:T(8,128)(2,1)} async-done(((bf16[4,256,2304]{2,1,0:T(8,128)(2,1)}), bf16[4,256,2304]{2,1,0:T(8,128)(2,1)}, u32[]{:S(2)}, u32[]{:S(2)}) %all-to-all-start) | async-done | bytes 4718624 | tf_op jit(solution)/shard_map/all_to_all | solution.py:226
  136.8 27.1 %shard_map.203 = bf16[1,1024,768]{2,1,0:T(8,128)(2,1)} custom-call(bf16[1,1024,2304]{2,1,0:T(8,128)(2,1)} %bitcast.3.q_ref.k_ref.v_ref, bf16[1,1024,2304]{2,1,0:T(8,128)(2,1)} %bitcast.3.q_ref.k_ref.v_ref, bf16[1,1024,2304]{2,1,0:T(8,128)(2,1)} %bitcast.3.q_ref.k_ref.v_ref, s32[1,1,1024]{2,1,0:T(1,128)S(1)} %get-tuple-element.105.row_ref, ...), custom_call_target="tpu_custom_call" | custom-call | flops 2415919104 | bytes 6291456 | tf_op jit(solution)/shard_map/pallas_call | solution.py:163
  163.9 8.4 %all-gather.6.cloned.1.call-done = bf16[768,1920]{1,0:T(8,128)(2,1)} async-done(((bf16[192,1920]{1,0:T(8,128)(2,1)}), bf16[768,1920]{1,0:T(8,128)(2,1)}) %all-gather.6.cloned.1.call-update) | async-done | bytes 2949136 | tf_op jit(solution)/shard_map/all_gather | solution.py:210
  173.1 4.6 all-to-all-start.1
  177.7 5.1 broadcast_select_fusion.3
  182.9 5.0 broadcast_select_fusion
  187.9 10.0 %all-to-all-done.1 = bf16[4,256,768]{2,1,0:T(8,128)(2,1)} async-done(((bf16[4,256,768]{2,1,0:T(8,128)(2,1)}), bf16[4,256,768]{2,1,0:T(8,128)(2,1)}, u32[]{:S(2)}, u32[]{:S(2)}) %all-to-all-start.1) | async-done | bytes 1572896 | tf_op jit(solution)/shard_map/all_to_all | solution.py:236
  204.3 8.5 %fusion.29 = f32[4,256,3072]{2,1,0:T(8,128)} fusion(bf16[768,1920]{1,0:T(8,128)(2,1)S(1)} %copy-done.16, bf16[768,1920]{1,0:T(8,128)(2,1)S(1)} %copy-done.15, f32[4,256,768]{2,1,0:T(8,128)S(1)} %get-tuple-element.109, f32[768]{0:T(1024)S(1)} %get-tuple-element.52, f32[768]{0:T(1024)S(1)} %get-tuple-element.50, f32[4,256]{1,0:T(4,128)S(1)} %fusion.43, ...), kind=kOutput, calls=%fused_computation.64 | convolution fusion | flops 4845207552 | bytes 21641216 | tf_op jit(solution)/shard_map/tyr,rw->tyw/dot_general | solution.py:355
  212.7 11.0 %bitcast_convert_fusion = bf16[3072,768]{1,0:T(8,128)(2,1)S(1)} fusion(bf16[4,256,768]{2,1,0:T(8,128)(2,1)S(1)} %copy-done.9, f32[4,256,3072]{2,1,0:T(8,128)} %fusion.29, f32[3072]{0:T(1024)S(1)} %add.293), kind=kOutput, calls=%fused_computation.14 | convolution fusion | flops 4865654784 | bytes 18886656 | tf_op jit(solution)/shard_map/ezg,ezv->gv/dot_general | solution.py:376
  223.8 18.8 %fusion.65 = (f32[3072]{0:T(1024)S(1)}, bf16[4,256,3072]{2,1,0:T(8,128)(2,1)}) fusion(f32[4,256,3072]{2,1,0:T(8,128)} %fusion.29, f32[3072]{0:T(1024)S(1)} %add.293, bf16[4,256,768]{2,1,0:T(8,128)(2,1)S(1)} %copy-done.9, bf16[3072,384]{1,0:T(8,128)(2,1)} %get-tuple-element.73, bf16[3072,384]{1,0:T(8,128)(2,1)S(1)} %copy-done.17), kind=kOutput, calls=%fused_computation.186 | convolution fusion | flops 4910478336 | bytes 25190400 | tf_op jit(solution)/shard_map/tuy,qy->tuq/dot_general | solution.py:379
  242.6 9.3 %multiply_reduce_fusion = (f32[768]{0:T(1024)S(1)}, f32[4,256]{1,0:T(4,128)S(1)}, f32[768]{0:T(1024)S(1)}, f32[4,256,768]{2,1,0:T(8,128)S(1)}) fusion(f32[4,256,768]{2,1,0:T(8,128)S(1)} %get-tuple-element.109, f32[4,256]{1,0:T(4,128)S(1)} %fusion.43, f32[4,256]{1,0:T(4,128)S(1)} %broadcast_multiply_fusion, f32[768]{0:T(1024)S(1)} %get-tuple-element.50, ...), kind=kOutput, calls=%fused_computation.50 | convolution fusion | flops 4847563776 | bytes 18502656 | tf_op jit(solution)/shard_map/naz,ez->nae/dot_general | solution.py:390
  251.9 9.9 %bitcast_convert_fusion.1 = bf16[768,3072]{1,0:T(8,128)(2,1)} fusion(bf16[4,256,3072]{2,1,0:T(8,128)(2,1)} %get-tuple-element.113, f32[4,256,768]{2,1,0:T(8,128)S(1)} %get-tuple-element.109, f32[768]{0:T(1024)S(1)} %get-tuple-element.52, f32[768]{0:T(1024)S(1)} %get-tuple-element.50, f32[4,256]{1,0:T(4,128)S(1)} %fusion.43, ...), kind=kOutput, calls=%fused_computation.15 | convolution fusion | flops 4838129664 | bytes 14170112 | tf_op jit(solution)/shard_map/zng,znw->gw/dot_general | solution.py:384
  264.8 4.4 convolution_convert_fusion
  274.5 4.5 all-to-all-start.2
  279.1 4.3 add_convert_fusion.1
  283.4 4.5 add_convert_fusion.2
  287.9 11.3 %all-to-all-done.2 = bf16[4,256,768]{2,1,0:T(8,128)(2,1)} async-done(((bf16[4,256,768]{2,1,0:T(8,128)(2,1)}), bf16[4,256,768]{2,1,0:T(8,128)(2,1)}, u32[]{:S(2)}, u32[]{:S(2)}) %all-to-all-start.2) | async-done | bytes 1572896 | tf_op jit(solution)/shard_map/all_to_all | solution.py:226
  299.2 38.7 %shard_map.204 = (bf16[1,1024,768]{2,1,0:T(8,128)(2,1)S(1)}, bf16[1,1024,768]{2,1,0:T(8,128)(2,1)S(1)}, bf16[1,1024,768]{2,1,0:T(8,128)(2,1)S(1)}) custom-call(bf16[1,1024,2304]{2,1,0:T(8,128)(2,1)} %bitcast.3.q_ref.k_ref.v_ref, bf16[1,1024,2304]{2,1,0:T(8,128)(2,1)} %bitcast.3.q_ref.k_ref.v_ref, bf16[1,1024,2304]{2,1,0:T(8,128)(2,1)} %bitcast.3.q_ref.k_ref.v_ref, ...), custom_call_target="tpu_custom_call" | custom-call | flops 5637144576 | bytes 11010048 | tf_op jit(solution)/shard_map/pallas_call | solution.py:183
  340.2 4.9 all-to-all-start.3
  352.4 22.6 %collective-permute-done.19 = bf16[4,192,768]{2,1,0:T(8,128)(2,1)} collective-permute-done((bf16[4,192,768]{2,1,0:T(8,128)(2,1)S(1)}, bf16[4,192,768]{2,1,0:T(8,128)(2,1)}, u32[]{:S(2)}, u32[]{:S(2)}) %collective-permute-start.19) | collective-permute-done | bytes 1179680 | tf_op jit(solution)/shard_map/ppermute | solution.py:201
  378.8 46.0 %collective-permute-done.17 = bf16[4,192,768]{2,1,0:T(8,128)(2,1)} collective-permute-done((bf16[4,192,768]{2,1,0:T(8,128)(2,1)}, bf16[4,192,768]{2,1,0:T(8,128)(2,1)}, u32[]{:S(2)}, u32[]{:S(2)}) %collective-permute-start.17) | collective-permute-done | bytes 1179680 | tf_op jit(solution)/shard_map/ppermute | solution.py:201
  444.7 7.0 %fusion.52 = (f32[768]{0:T(1024)S(1)}, f32[4,256]{1,0:T(4,128)S(1)}, f32[4,256,768]{2,1,0:T(8,128)S(1)}) fusion(f32[768]{0:T(1024)S(1)} %get-tuple-element.57, f32[4,256]{1,0:T(4,128)S(1)} %broadcast_multiply_fusion.1, bf16[4,256,768]{2,1,0:T(8,128)(2,1)S(1)} %copy-done.2, bf16[4,256,2304]{2,1,0:T(8,128)(2,1)} %all-to-all-done.3, ...), kind=kOutput, calls=%fused_computation.178 | convolution fusion | flops 3635673344 | bytes 12990464 | tf_op jit(solution)/shard_map/wri,yi->wry/dot_general | solution.py:442
  460.1 6.8 %bitcast_convert_fusion.2 = bf16[768,2304]{1,0:T(8,128)(2,1)S(1)} fusion(bf16[4,256,2304]{2,1,0:T(8,128)(2,1)} %all-to-all-done.3, bf16[4,256,768]{2,1,0:T(8,128)(2,1)S(1)} %copy-done.2, f32[768]{0:T(1024)S(1)} %get-tuple-element.56, f32[768]{0:T(1024)S(1)} %get-tuple-element.57, f32[4,256]{1,0:T(4,128)S(1)} %fusion.42, ...), kind=kOutput, calls=%fused_computation.18 | convolution fusion | flops 3630366720 | bytes 9844736 | tf_op jit(solution)/shard_map/azk,azx->kx/dot_general | solution.py:439
  480.7 12.0 %add_convert_fusion.3 = bf16[4,256,768]{2,1,0:T(8,128)(2,1)} fusion(f32[4,256,768]{2,1,0:T(8,128)S(1)} %copy-done.4, f32[768]{0:T(1024)S(1)} %copy-done.31, bf16[3072,384]{1,0:T(8,128)(2,1)S(1)} %copy-done.19, bf16[3072,384]{1,0:T(8,128)(2,1)S(1)} %copy-done.18, f32[4,256,3072]{2,1,0:T(8,128)} %fusion.29, f32[3072]{0:T(1024)S(1)} %add.293), kind=kOutput, calls=%fused_computation.56 | convolution fusion | flops 4875091968 | bytes 22035456 | tf_op jit(solution)/shard_map/crx,xo->cro/dot_general | solution.py:366
  503.6 9.0 %collective-permute-done.6 = bf16[4,192,384]{2,1,0:T(8,128)(2,1)S(1)} collective-permute-done((bf16[4,192,384]{2,1,0:T(8,128)(2,1)S(1)}, bf16[4,192,384]{2,1,0:T(8,128)(2,1)S(1)}, u32[]{:S(2)}, u32[]{:S(2)}) %collective-permute-start.6) | collective-permute-done | bytes 589856 | tf_op jit(solution)/shard_map/ppermute | solution.py:201
  518.8 6.4 %collective-permute-done.7 = bf16[4,192,192]{2,1,0:T(8,128)(2,1)S(1)} collective-permute-done((bf16[4,192,192]{2,1,0:T(8,128)(2,1)S(1)}, bf16[4,192,192]{2,1,0:T(8,128)(2,1)S(1)}, u32[]{:S(2)}, u32[]{:S(2)}) %collective-permute-start.7) | collective-permute-done | bytes 294944 | tf_op jit(solution)/shard_map/ppermute | solution.py:201
  534.5 12.9 %reduce-scatter.3.cloned.1.call-done = bf16[1,192,384]{2,1,0:T(8,128)(2,1)} async-done(((bf16[4,192,384]{2,1,0:T(8,128)(2,1)}), bf16[1,192,384]{2,1,0:T(8,128)(2,1)}) %reduce-scatter.3.cloned.1.call-update) | async-done | bytes 147472 | tf_op jit(solution)/shard_map/reduce_scatter | solution.py:272
  556.6 6.7 %multiply_subtract_fusion.1 = (f32[768,768]{1,0:T(8,128)}, f32[768,768]{1,0:T(8,128)}, f32[768,768]{1,0:T(8,128)}) fusion(f32[768,768]{1,0:T(8,128)} %param.18, bf16[384,768]{1,0:T(8,128)(2,1)S(1)} %get-tuple-element.79, bf16[384,768]{1,0:T(8,128)(2,1)S(1)} %get-tuple-element.78, f32[768,768]{1,0:T(8,128)S(1)} %copy-done.20, f32[768,768]{1,0:T(8,128)} %param.20), kind=kLoop, calls=%fused_computation.69 | loop fusion | flops 11206656 | bytes 15335424 | tf_op jit(solution)/shard_map/sub | solution.py:40
  570.9 8.7 %multiply_subtract_fusion = (f32[192,6144]{1,0:T(8,128)}, f32[192,6144]{1,0:T(8,128)}, f32[192,6144]{1,0:T(8,128)}) fusion(f32[192,6144]{1,0:T(8,128)S(1)} %bitcast.78, bf16[192,6144]{1,0:T(8,128)(2,1)S(1)} %select_dynamic-update-slice_fusion, f32[192,6144]{1,0:T(8,128)} %param.16, f32[192,6144]{1,0:T(8,128)} %param.17), kind=kLoop, calls=%fused_computation.36 | loop fusion | flops 18874368 | bytes 30670848 | tf_op jit(solution)/shard_map/sub | solution.py:40
  (251 shorter events, 134.6 us)
Async XLA Ops:
  7.2 52.3 %all-gather.4.cloned.1.call-start = ((), (), s32[]{:S(2)}) async-start(), calls=%async_computation.6 | async-start | bytes 2457600 | tf_op jit(solution)/shard_map/all_gather | solution.py:311
  13.1 150.8 %all-gather.8.cloned.1.call-start = ((), (), s32[]{:S(2)}) async-start(), calls=%async_computation.8 | async-start | bytes 2949120 | tf_op jit(solution)/shard_map/all_gather | solution.py:210
  60.4 111.8 %all-gather.6.cloned.1.call-start = ((), (), s32[]{:S(2)}) async-start(), calls=%async_computation.7 | async-start | bytes 3686400 | tf_op jit(solution)/shard_map/all_gather | solution.py:210
  78.0 58.8 %all-to-all-start = ((bf16[4,256,2304]{2,1,0:T(8,128)(2,1)}), bf16[4,256,2304]{2,1,0:T(8,128)(2,1)}, u32[]{:S(2)}, u32[]{:S(2)}) async-start(bf16[4,256,2304]{2,1,0:T(8,128)(2,1)} %add_convert_fusion), calls=%async_computation | async-start | bytes 9437184 | tf_op jit(solution)/shard_map/all_to_all | solution.py:226
  172.3 5.4 collective-permute-start.2
  172.3 10.6 %collective-permute-start.1 = (bf16[768,1920]{1,0:T(8,128)(2,1)}, bf16[768,1920]{1,0:T(8,128)(2,1)}, u32[]{:S(2)}, u32[]{:S(2)}) collective-permute-start(bf16[768,1920]{1,0:T(8,128)(2,1)} %all-gather.6.cloned.1.call-done), channel_id=1, source_target_pairs={{0,8},{8,0},{16,24},{24,16},{1,9},{9,1},{17,25},{25,17},{2,10},{10... | collective-permute-start | bytes 8847368 | tf_op jit(solution)/shard_map/ppermute | solution.py:201
  173.1 24.7 %all-to-all-start.1 = ((bf16[4,256,768]{2,1,0:T(8,128)(2,1)}), bf16[4,256,768]{2,1,0:T(8,128)(2,1)}, u32[]{:S(2)}, u32[]{:S(2)}) async-start(bf16[4,256,768]{2,1,0:T(8,128)(2,1)} %bitcast.6), calls=%async_computation.1 | async-start | bytes 3145728 | tf_op jit(solution)/shard_map/all_to_all | solution.py:236
  270.7 8.4 %collective-permute-start.4 = (bf16[4,384,768]{2,1,0:T(8,128)(2,1)}, bf16[4,384,768]{2,1,0:T(8,128)(2,1)}, u32[]{:S(2)}, u32[]{:S(2)}) collective-permute-start(bf16[4,384,768]{2,1,0:T(8,128)(2,1)} %constant_dynamic-slice_fusion.10), channel_id=1, source_target_pairs={{0,8},{8,0},{16,24},{24,16},{1,9},{9,1},{17,25},{25,17},{2,10},{10... | collective-permute-start | bytes 7077896 | tf_op jit(solution)/shard_map/ppermute | solution.py:201
  274.0 9.4 %collective-permute-start.3 = (bf16[4,192,1536]{2,1,0:T(8,128)(2,1)}, bf16[4,192,1536]{2,1,0:T(8,128)(2,1)}, u32[]{:S(2)}, u32[]{:S(2)}) collective-permute-start(bf16[4,192,1536]{2,1,0:T(8,128)(2,1)} %constant_dynamic-slice_fusion.11), channel_id=1, source_target_pairs={{0,8},{8,0},{16,24},{24,16},{1,9},{9,1},{17,25},{25,17},{2,10},{10... | collective-permute-start | bytes 7077896 | tf_op jit(solution)/shard_map/ppermute | solution.py:201
  274.5 24.7 %all-to-all-start.2 = ((bf16[4,256,768]{2,1,0:T(8,128)(2,1)}), bf16[4,256,768]{2,1,0:T(8,128)(2,1)}, u32[]{:S(2)}, u32[]{:S(2)}) async-start(bf16[4,256,768]{2,1,0:T(8,128)(2,1)} %convolution_convert_fusion), calls=%async_computation.2 | async-start | bytes 3145728 | tf_op jit(solution)/shard_map/all_to_all | solution.py:226
  340.2 104.4 %all-to-all-start.3 = ((bf16[4,256,2304]{2,1,0:T(8,128)(2,1)}), bf16[4,256,2304]{2,1,0:T(8,128)(2,1)}, u32[]{:S(2)}, u32[]{:S(2)}) async-start(bf16[4,256,2304]{2,1,0:T(8,128)(2,1)} %bitcast.76), calls=%async_computation.3 | async-start | bytes 9437184 | tf_op jit(solution)/shard_map/all_to_all | solution.py:236
  345.2 148.3 %reduce-scatter.5.cloned.1.call-start = ((), (), s32[]{:S(2)}) async-start(), calls=%async_computation.10 | async-start | bytes 1474560 | tf_op jit(solution)/shard_map/reduce_scatter | solution.py:272
  346.6 28.5 %collective-permute-start.19 = (bf16[4,192,768]{2,1,0:T(8,128)(2,1)S(1)}, bf16[4,192,768]{2,1,0:T(8,128)(2,1)}, u32[]{:S(2)}, u32[]{:S(2)}) collective-permute-start(bf16[4,192,768]{2,1,0:T(8,128)(2,1)S(1)} %constant_dynamic-slice_fusion.1), channel_id=1, source_target_pairs={{0,1},{1,0},{2,3},{3,2},{4,5},{5,4},{6,7},{7,6},{8,9},{9,8},{10,11... | collective-permute-start | bytes 3538952 | tf_op jit(solution)/shard_map/ppermute | solution.py:201
  350.5 74.3 %collective-permute-start.17 = (bf16[4,192,768]{2,1,0:T(8,128)(2,1)}, bf16[4,192,768]{2,1,0:T(8,128)(2,1)}, u32[]{:S(2)}, u32[]{:S(2)}) collective-permute-start(bf16[4,192,768]{2,1,0:T(8,128)(2,1)} %constant_dynamic-slice_fusion.3), channel_id=1, source_target_pairs={{0,16},{8,24},{16,0},{24,8},{1,17},{9,25},{17,1},{25,9},{2,18},{10... | collective-permute-start | bytes 3538952 | tf_op jit(solution)/shard_map/ppermute | solution.py:201
  377.1 59.9 %collective-permute-start.20 = (bf16[4,96,768]{2,1,0:T(8,128)(2,1)S(1)}, bf16[4,96,768]{2,1,0:T(8,128)(2,1)}, u32[]{:S(2)}, u32[]{:S(2)}) collective-permute-start(bf16[4,96,768]{2,1,0:T(8,128)(2,1)S(1)} %constant_dynamic-slice_fusion), channel_id=1, source_target_pairs={{0,16},{8,24},{16,0},{24,8},{1,17},{9,25},{17,1},{25,9},{2,18},{10... | collective-permute-start | bytes 1769480 | tf_op jit(solution)/shard_map/ppermute | solution.py:201
  427.3 14.7 %collective-permute-start.18 = (bf16[4,192,384]{2,1,0:T(8,128)(2,1)}, bf16[4,192,384]{2,1,0:T(8,128)(2,1)}, u32[]{:S(2)}, u32[]{:S(2)}) collective-permute-start(bf16[4,192,384]{2,1,0:T(8,128)(2,1)} %constant_dynamic-slice_fusion.2), channel_id=1, source_target_pairs={{0,1},{1,0},{2,3},{3,2},{4,5},{5,4},{6,7},{7,6},{8,9},{9,8},{10,11... | collective-permute-start | bytes 1769480 | tf_op jit(solution)/shard_map/ppermute | solution.py:201
  444.4 103.0 %reduce-scatter.3.cloned.1.call-start = ((), (), s32[]{:S(2)}) async-start(), calls=%async_computation.9 | async-start | bytes 737280 | tf_op jit(solution)/shard_map/reduce_scatter | solution.py:272
  460.1 6.9 %collective-permute-start.27 = (f32[12,768]{1,0:T(8,128)S(1)}, f32[12,768]{1,0:T(8,128)S(1)}, u32[]{:S(2)}, u32[]{:S(2)}) collective-permute-start(f32[12,768]{1,0:T(8,128)S(1)} %concatenate.88), channel_id=1, source_target_pairs={{0,8},{8,0},{16,24},{24,16},{1,9},{9,1},{17,25},{25,17},{2,10},{10... | collective-permute-start | bytes 110600 | tf_op jit(solution)/shard_map/ppermute | solution.py:201
  475.5 22.0 %collective-permute-start.5 = (bf16[4,192,768]{2,1,0:T(8,128)(2,1)S(1)}, bf16[4,192,768]{2,1,0:T(8,128)(2,1)}, u32[]{:S(2)}, u32[]{:S(2)}) collective-permute-start(bf16[4,192,768]{2,1,0:T(8,128)(2,1)S(1)} %constant_dynamic-slice_fusion.9), channel_id=1, source_target_pairs={{0,8},{8,0},{16,24},{24,16},{1,9},{9,1},{17,25},{25,17},{2,10},{10... | collective-permute-start | bytes 3538952 | tf_op jit(solution)/shard_map/ppermute | solution.py:201
  475.6 25.4 %collective-permute-start.8 = (bf16[4,192,768]{2,1,0:T(8,128)(2,1)S(1)}, bf16[4,192,768]{2,1,0:T(8,128)(2,1)}, u32[]{:S(2)}, u32[]{:S(2)}) collective-permute-start(bf16[4,192,768]{2,1,0:T(8,128)(2,1)S(1)} %constant_dynamic-slice_fusion.6), channel_id=1, source_target_pairs={{0,8},{8,0},{16,24},{24,16},{1,9},{9,1},{17,25},{25,17},{2,10},{10... | collective-permute-start | bytes 3538952 | tf_op jit(solution)/shard_map/ppermute | solution.py:201
  479.5 13.2 %collective-permute-start.31 = (f32[12,768]{1,0:T(8,128)S(1)}, f32[12,768]{1,0:T(8,128)S(1)}, u32[]{:S(2)}, u32[]{:S(2)}) collective-permute-start(f32[12,768]{1,0:T(8,128)S(1)} %add.346), channel_id=1, source_target_pairs={{0,4},{2,6},{4,0},{6,2},{1,5},{3,7},{5,1},{7,3},{8,12},{10,14},{12... | collective-permute-start | bytes 110600 | tf_op jit(solution)/shard_map/ppermute | solution.py:201
  495.4 8.2 %collective-permute-start.24 = (bf16[96,768]{1,0:T(8,128)(2,1)S(1)}, bf16[96,768]{1,0:T(8,128)(2,1)S(1)}, u32[]{:S(2)}, u32[]{:S(2)}) collective-permute-start(bf16[96,768]{1,0:T(8,128)(2,1)S(1)} %pad_maximum_fusion.13), channel_id=1, source_target_pairs={{0,16},{8,24},{16,0},{24,8},{1,17},{9,25},{17,1},{25,9},{2,18},{10... | collective-permute-start | bytes 442376 | tf_op jit(solution)/shard_map/ppermute | solution.py:201
  496.0 30.6 %collective-permute-start.21 = (bf16[192,384]{1,0:T(8,128)(2,1)S(1)}, bf16[192,384]{1,0:T(8,128)(2,1)S(1)}, u32[]{:S(2)}, u32[]{:S(2)}) collective-permute-start(bf16[192,384]{1,0:T(8,128)(2,1)S(1)} %slice.128), channel_id=1, source_target_pairs={{0,1},{1,0},{2,3},{3,2},{4,5},{5,4},{6,7},{7,6},{8,9},{9,8},{10,11... | collective-permute-start | bytes 442376 | tf_op jit(solution)/shard_map/ppermute | solution.py:201
  499.5 13.2 %collective-permute-start.6 = (bf16[4,192,384]{2,1,0:T(8,128)(2,1)S(1)}, bf16[4,192,384]{2,1,0:T(8,128)(2,1)S(1)}, u32[]{:S(2)}, u32[]{:S(2)}) collective-permute-start(bf16[4,192,384]{2,1,0:T(8,128)(2,1)S(1)} %constant_dynamic-slice_fusion.8), channel_id=1, source_target_pairs={{0,16},{8,24},{16,0},{24,8},{1,17},{9,25},{17,1},{25,9},{2,18},{10... | collective-permute-start | bytes 1769480 | tf_op jit(solution)/shard_map/ppermute | solution.py:201
  503.0 13.3 %collective-permute-start.9 = (bf16[4,192,384]{2,1,0:T(8,128)(2,1)S(1)}, bf16[4,192,384]{2,1,0:T(8,128)(2,1)S(1)}, u32[]{:S(2)}, u32[]{:S(2)}) collective-permute-start(bf16[4,192,384]{2,1,0:T(8,128)(2,1)S(1)} %constant_dynamic-slice_fusion.5), channel_id=1, source_target_pairs={{0,1},{1,0},{2,3},{3,2},{4,5},{5,4},{6,7},{7,6},{8,9},{9,8},{10,11... | collective-permute-start | bytes 1769480 | tf_op jit(solution)/shard_map/ppermute | solution.py:201
  513.0 12.1 %collective-permute-start.7 = (bf16[4,192,192]{2,1,0:T(8,128)(2,1)S(1)}, bf16[4,192,192]{2,1,0:T(8,128)(2,1)S(1)}, u32[]{:S(2)}, u32[]{:S(2)}) collective-permute-start(bf16[4,192,192]{2,1,0:T(8,128)(2,1)S(1)} %constant_dynamic-slice_fusion.7), channel_id=1, source_target_pairs={{0,1},{1,0},{2,3},{3,2},{4,5},{5,4},{6,7},{7,6},{8,9},{9,8},{10,11... | collective-permute-start | bytes 884744 | tf_op jit(solution)/shard_map/ppermute | solution.py:201
  516.6 8.7 %collective-permute-start.10 = (bf16[4,192,192]{2,1,0:T(8,128)(2,1)S(1)}, bf16[4,192,192]{2,1,0:T(8,128)(2,1)S(1)}, u32[]{:S(2)}, u32[]{:S(2)}) collective-permute-start(bf16[4,192,192]{2,1,0:T(8,128)(2,1)S(1)} %constant_dynamic-slice_fusion.4), channel_id=1, source_target_pairs={{0,16},{8,24},{16,0},{24,8},{1,17},{9,25},{17,1},{25,9},{2,18},{10... | collective-permute-start | bytes 884744 | tf_op jit(solution)/shard_map/ppermute | solution.py:201
  517.3 11.9 %collective-permute-start.25 = (bf16[192,768]{1,0:T(8,128)(2,1)S(1)}, bf16[192,768]{1,0:T(8,128)(2,1)S(1)}, u32[]{:S(2)}, u32[]{:S(2)}) collective-permute-start(bf16[192,768]{1,0:T(8,128)(2,1)S(1)} %pad_maximum_fusion.10), channel_id=1, source_target_pairs={{0,1},{1,0},{2,3},{3,2},{4,5},{5,4},{6,7},{7,6},{8,9},{9,8},{10,11... | collective-permute-start | bytes 884744 | tf_op jit(solution)/shard_map/ppermute | solution.py:201
  526.7 6.8 %collective-permute-start.22 = (bf16[192,768]{1,0:T(8,128)(2,1)S(1)}, bf16[192,768]{1,0:T(8,128)(2,1)S(1)}, u32[]{:S(2)}, u32[]{:S(2)}) collective-permute-start(bf16[192,768]{1,0:T(8,128)(2,1)S(1)} %pad_maximum_fusion.9), channel_id=1, source_target_pairs={{0,16},{8,24},{16,0},{24,8},{1,17},{9,25},{17,1},{25,9},{2,18},{10... | collective-permute-start | bytes 884744 | tf_op jit(solution)/shard_map/ppermute | solution.py:201
  530.2 21.3 %collective-permute-start.26 = (bf16[384,768]{1,0:T(8,128)(2,1)}, bf16[384,768]{1,0:T(8,128)(2,1)S(1)}, u32[]{:S(2)}, u32[]{:S(2)}) collective-permute-start(bf16[384,768]{1,0:T(8,128)(2,1)} %pad_maximum_fusion.6), channel_id=1, source_target_pairs={{0,8},{8,0},{16,24},{24,16},{1,9},{9,1},{17,25},{25,17},{2,10},{10... | collective-permute-start | bytes 1769480 | tf_op jit(solution)/shard_map/ppermute | solution.py:201
  534.5 36.1 %collective-permute-start.23 = (bf16[192,1536]{1,0:T(8,128)(2,1)}, bf16[192,1536]{1,0:T(8,128)(2,1)S(1)}, u32[]{:S(2)}, u32[]{:S(2)}) collective-permute-start(bf16[192,1536]{1,0:T(8,128)(2,1)} %pad_maximum_fusion.5), channel_id=1, source_target_pairs={{0,8},{8,0},{16,24},{24,16},{1,9},{9,1},{17,25},{25,17},{2,10},{10... | collective-permute-start | bytes 1769480 | tf_op jit(solution)/shard_map/ppermute | solution.py:201
  555.8 9.0 %collective-permute-start.12 = (bf16[192,384]{1,0:T(8,128)(2,1)S(1)}, bf16[192,384]{1,0:T(8,128)(2,1)S(1)}, u32[]{:S(2)}, u32[]{:S(2)}) collective-permute-start(bf16[192,384]{1,0:T(8,128)(2,1)S(1)} %pad_maximum_fusion.11), channel_id=1, source_target_pairs={{0,16},{8,24},{16,0},{24,8},{1,17},{9,25},{17,1},{25,9},{2,18},{10... | collective-permute-start | bytes 442376 | tf_op jit(solution)/shard_map/ppermute | solution.py:201
  (44 other events, 583.1 us)
Sparse Core Ops, SparseCore 0:
  13.2 46.2 all-gather.3
  61.7 49.3 all-gather.7
  113.2 59.0 all-gather.5
  444.5 26.9 reduce-scatter.4
  526.8 20.6 reduce-scatter.2

commit v3 on v2

--- a/solution.py
+++ b/solution.py
@@ -155,33 +155,33 @@
     return column, row, col
 
 
-def attend(mixed, rows, cols):
+def attend(mixed, rows, cols, head_width):
     count, length, width = mixed.shape
     width //= 3
     groups = width // LANES
     column, row, col = attention_specs(length, groups)
     return pl.pallas_call(
-        functools.partial(attend_kernel, width // H),
+        functools.partial(attend_kernel, head_width),
         grid=(count, groups),
         in_specs=[column(0), column(1), column(2), row, col],
         out_specs=column(0),
         out_shape=jax.ShapeDtypeStruct((count, length, width), jnp.bfloat16),
         compiler_params=pltpu.CompilerParams(vmem_limit_bytes=48 * 2**20),
         cost_estimate=pl.CostEstimate(
-            flops=3 * count * length * length * width,
+            flops=12 * count * length * length * width,
             bytes_accessed=8 * count * length * width,
-            transcendentals=count * H * length * length // 2,
+            transcendentals=count * (width // head_width) * length * length // 2,
         ),
     )(mixed, mixed, mixed, rows, cols)
 
 
-def attend_back(mixed, grads, rows, cols):
+def attend_back(mixed, grads, rows, cols, head_width):
     count, length, width = grads.shape
     groups = width // LANES
     column, row, col = attention_specs(length, groups)
     shape = jax.ShapeDtypeStruct((count, length, width), jnp.bfloat16)
     return pl.pallas_call(
-        functools.partial(attend_back_kernel, width // H),
+        functools.partial(attend_back_kernel, head_width),
         grid=(count, groups),
         in_specs=[column(0), column(1), column(2), column(0), row, col],
         out_specs=[column(0)] * 3,
@@ -189,9 +189,9 @@
         scratch_shapes=[pltpu.VMEM((length, LANES), jnp.float32)] * 2,
         compiler_params=pltpu.CompilerParams(vmem_limit_bytes=48 * 2**20),
         cost_estimate=pl.CostEstimate(
-            flops=7 * count * length * length * width,
+            flops=40 * count * length * length * width,
             bytes_accessed=14 * count * length * width,
-            transcendentals=count * H * length * length // 2,
+            transcendentals=count * (width // head_width) * length * length // 2,
         ),
     )(mixed, mixed, mixed, grads, rows, cols)
 
@@ -234,6 +234,13 @@
     values = jnp.moveaxis(values.reshape(count, size, length // size, width), 1, 0)
     values = values.reshape(size * count, length // size, width)
     return lax.all_to_all(values, "seq", split_axis=0, concat_axis=0, tiled=True)
+
+
+def side_by_side(parts, kinds):
+    return jnp.concatenate(
+        [piece for row in zip(*(jnp.split(part, kinds, axis=-1) for part in parts)) for piece in row],
+        axis=-1,
+    )
 
 
 def butterfly_sum(values, axes):
@@ -326,17 +333,29 @@
         "rxj,jw->rxw", normalized_block, matrix_qkv, preferred_element_type=jnp.float32
     )
     bias = jnp.concatenate([small_vals[2], jnp.zeros_like(small_vals[2]), small_vals[3]])
-    mixed = to_sequences((projected + bias).astype(jnp.bfloat16))
-    own_count = mixed.shape[0]
+    projected = (projected + bias).astype(jnp.bfloat16)
+    head_width = model_width // H
+    middle_column = model_width // 2
+    halves = [slice(0, middle_column), slice(middle_column, model_width)]
+    kinds = jnp.split(projected, 3, axis=-1)
+    mixed = [
+        to_sequences(jnp.concatenate([kind[..., half] for kind in kinds], axis=-1))
+        for half in halves
+    ]
+    own_count = mixed[0].shape[0]
     own_segments = lax.dynamic_slice_in_dim(
         segments, lax.axis_index("seq") * own_count, own_count, 0
     )
     segment_rows = own_segments[:, None, :]
     segment_cols = own_segments[:, :, None]
-    attended_own, half_rest, half_down = lax.optimization_barrier(
-        (attend(mixed, segment_rows, segment_cols), half_rest, half_down)
-    )
-    attended_block = to_pieces(attended_own)
+    attended_first = attend(mixed[0], segment_rows, segment_cols, head_width)
+    attended_first, second_mixed = lax.optimization_barrier((attended_first, mixed[1]))
+    attended_second, half_rest, half_down = lax.optimization_barrier(
+        (attend(second_mixed, segment_rows, segment_cols, head_width), half_rest, half_down)
+    )
+    attended_block = jnp.concatenate(
+        [to_pieces(attended_first), to_pieces(attended_second)], axis=-1
+    )
     matrix_rest = swap_halves(half_rest)
     matrix_down = swap_halves(half_down)
     matrix_out = matrix_rest[:, :model_width]
@@ -415,11 +434,32 @@
     first, rest, replicas = plane_steps()
     part_up = halve_all(by_owner(grad_up), first, 2)
     part_down = halve_all(by_owner(down_weight_gradient), first, 1)
-    grad_attended_own, part_up, part_down = lax.optimization_barrier(
-        (to_sequences(grad_attended_b), part_up, part_down)
-    )
-    part_up = halve_all(part_up, rest + replicas, 2)
-    part_down = halve_all(part_down, replicas + rest, 1)
+    grad_first, grad_second, part_up, part_down = lax.optimization_barrier(
+        (
+            to_sequences(grad_attended_b[..., halves[0]]),
+            to_sequences(grad_attended_b[..., halves[1]]),
+            part_up,
+            part_down,
+        )
+    )
+    back_first = attend_back(mixed[0], grad_first, segment_rows, segment_cols, head_width)
+    back_first, grad_second, part_up, part_down = lax.optimization_barrier(
+        (
+            jnp.concatenate(back_first, axis=-1),
+            grad_second,
+            halve_all(part_up, rest, 2),
+            halve_all(part_down, replicas, 1),
+        )
+    )
+    mixed_first = to_pieces(back_first)
+    back_second = attend_back(mixed[1], grad_second, segment_rows, segment_cols, head_width)
+    back_second, part_up, part_down = lax.optimization_barrier(
+        (
+            jnp.concatenate(back_second, axis=-1),
+            halve_all(part_up, replicas, 2),
+            halve_all(part_down, rest, 1),
+        )
+    )
     up_columns = part_up.shape[2]
     part_down = jnp.concatenate(
         [part_down[:, :, :up_columns], part_down[:, :, up_columns:]], axis=1
@@ -433,8 +473,7 @@
         first + replicas + rest,
         0,
     ).astype(jnp.float32)
-    grad_mixed = attend_back(mixed, grad_attended_own, segment_rows, segment_cols)
-    mixed_block_gradient = to_pieces(jnp.concatenate(grad_mixed, axis=-1))
+    mixed_block_gradient = side_by_side([mixed_first, to_pieces(back_second)], 3)
     mixed_sums = over_tokens(mixed_block_gradient.astype(jnp.float32))
     query_key_value_gradient = jnp.einsum(
         "azk,azx->kx", normalized_block, mixed_block_gradient, preferred_element_type=jnp.float32

time: 595 us -> 588 us (0.988)
  waiting for transfers between devices: 256 us -> 199 us
  local copies, waits for them, and re-layouts: 29 us -> 58 us
  blocking collectives: 0 us -> 14.7 us
  starting transfers between devices: 44.7 us -> 52.7 us
    ppermute x32, waiting for transfers between devices: 116 us -> 53.7 us  [partner(): return lax.ppermute(values, axis, [(i, i ^ bit) for i in range(size)])]
    unnamed x68 -> x134, local copies, waits for them, and re-layouts: 7.65 us -> 22.7 us
    all_to_all x0 -> x1, blocking collectives: none -> 14.7 us  [to_pieces(): lax.all_to_all(values, 'seq', split_axis=0, concat_axis=0, tiled=True)]
    all_to_all x2 -> x3, waiting for transfers between devices: 9.97 us -> 24.5 us  [to_pieces(): lax.all_to_all(values, 'seq', split_axis=0, concat_axis=0, tiled=True)]
    all_to_all x2 -> x4, waiting for transfers between devices: 64.2 us -> 50.7 us  [to_sequences(): lax.all_to_all(values, 'seq', split_axis=0, concat_axis=0, tiled=True)]
    all_to_all x2 -> x4, starting transfers between devices: 9.49 us -> 15.3 us  [to_sequences(): lax.all_to_all(values, 'seq', split_axis=0, concat_axis=0, tiled=True)]
    all_to_all x2 -> x3, starting transfers between devices: 9.52 us -> 12.1 us  [to_pieces(): lax.all_to_all(values, 'seq', split_axis=0, concat_axis=0, tiled=True)]
    pallas_call x2 -> x4, Pallas kernels: 65.7 us -> 65.7 us  [the longest x2 39 us: attend_back(): pl.pallas_call(functools.partial(attend_back_kernel, head_width), grid=(c...]
  transfers between devices with their start and end apart: 41 -> 44, of which waited for: 22 -> 23; matrix products, arithmetic and copies ran while one was open for 19% -> 22% of each run, Pallas kernels for 5% -> 11%
where the time goes in v3:
time: 588 us; the launch traced here: 579 us
  waiting for transfers between devices  199 us (34%)
  matrix products  99 us (17%)
  other arithmetic  74.8 us (13%)
  Pallas kernels  65.7 us (11%)
  local copies, waits for them, and re-layouts  58 us (10%)
  starting transfers between devices  52.7 us (9%)
  between operations  15.2 us (3%)
  blocking collectives  14.7 us (2%)
    ppermute x32, waiting for transfers between devices, partner(): return lax.ppermute(values, axis, [(i, i ^ bit) for i in range(size)])  53.7 us
    all_to_all x4, waiting for transfers between devices, to_sequences(): lax.all_to_all(values, 'seq', split_axis=0, concat_axis=0, tiled=True)  50.7 us
    all_gather x1, waiting for transfers between devices, body(): lax.all_gather(jnp.concatenate([own_qkv, small_pad], axis=1), 'fsdp', axi...  44.2 us
    pallas_call x2, Pallas kernels, attend_back(): pl.pallas_call(functools.partial(attend_back_kernel, head_width), grid=(c...  39 us
    pallas_call x2, Pallas kernels, attend(): pl.pallas_call(functools.partial(attend_kernel, head_width), grid=(count,...  26.7 us
    ppermute x32, starting transfers between devices, partner(): return lax.ppermute(values, axis, [(i, i ^ bit) for i in range(size)])  24.7 us
    all_to_all x3, waiting for transfers between devices, to_pieces(): lax.all_to_all(values, 'seq', split_axis=0, concat_axis=0, tiled=True)  24.5 us
    unnamed x134, local copies, waits for them, and re-layouts  22.7 us
  transfers between devices with their start and end apart: 44, of which 23 were waited for; matrix products, arithmetic and copies ran while one was open for 22% of the time, Pallas kernels for 11%

profile of v3, /device:TPU:0, one launch (start us, length us, event | category | flops | bytes accessed | tf_op | source)
XLA Modules:
  0.0 579.2 jit_solution(16304703628031585459)
XLA Ops:
  14.1 44.2 %all-gather.4.cloned.1.call-done = bf16[768,1280]{1,0:T(8,128)(2,1)} async-done(((bf16[192,1280]{1,0:T(8,128)(2,1)}), bf16[768,1280]{1,0:T(8,128)(2,1)}) %all-gather.4.cloned.1.call-update) | async-done | bytes 1966096 | tf_op jit(solution)/shard_map/all_gather | solution.py:318
  83.9 25.5 %all-to-all-done = bf16[4,256,1152]{2,1,0:T(8,128)(2,1)S(1)} async-done(((bf16[4,256,1152]{2,1,0:T(8,128)(2,1)}), bf16[4,256,1152]{2,1,0:T(8,128)(2,1)S(1)}, u32[]{:S(2)}, u32[]{:S(2)}) %all-to-all-start) | async-done | bytes 2359328 | tf_op jit(solution)/shard_map/all_to_all | solution.py:226
  119.3 13.0 %shard_map.203 = bf16[1,1024,384]{2,1,0:T(8,128)(2,1)S(1)} custom-call(bf16[1,1024,1152]{2,1,0:T(8,128)(2,1)S(1)} %bitcast.86, bf16[1,1024,1152]{2,1,0:T(8,128)(2,1)S(1)} %bitcast.87, bf16[1,1024,1152]{2,1,0:T(8,128)(2,1)S(1)} %bitcast.88, s32[1,1,1024]{2,1,0:T(1,128)S(1)} %get-tuple-element.139.row_ref, s32[1,1024,1]{2,1,0:T(8,128)S(1)} %copy-done.3), custom_call_target="tpu_custom_call" | custom-call | flops 4831838208 | bytes 3145728 | tf_op jit(solution)/shard_map/pallas_call | solution.py:163
  132.4 10.7 %all-to-all-done.1 = bf16[4,256,1152]{2,1,0:T(8,128)(2,1)S(1)} async-done(((bf16[4,256,1152]{2,1,0:T(8,128)(2,1)}), bf16[4,256,1152]{2,1,0:T(8,128)(2,1)S(1)}, u32[]{:S(2)}, u32[]{:S(2)}) %all-to-all-start.1) | async-done | bytes 2359328 | tf_op jit(solution)/shard_map/all_to_all | solution.py:226
  144.1 13.7 %shard_map.204 = bf16[1,1024,384]{2,1,0:T(8,128)(2,1)} custom-call(bf16[1,1024,1152]{2,1,0:T(8,128)(2,1)S(1)} %bitcast.80, bf16[1,1024,1152]{2,1,0:T(8,128)(2,1)S(1)} %bitcast.81, bf16[1,1024,1152]{2,1,0:T(8,128)(2,1)S(1)} %bitcast.82, s32[1,1,1024]{2,1,0:T(1,128)S(1)} %get-tuple-element.139.row_ref, s32[1,1024,1]{2,1,0:T(8,128)S(1)} %copy-done.4), custom_call_target="tpu_custom_call" | custom-call | flops 4831838208 | bytes 3145728 | tf_op jit(solution)/shard_map/pallas_call | solution.py:163
  157.8 13.2 %all-gather.6.cloned.1.call-done = bf16[768,1920]{1,0:T(8,128)(2,1)} async-done(((bf16[192,1920]{1,0:T(8,128)(2,1)}), bf16[768,1920]{1,0:T(8,128)(2,1)}) %all-gather.6.cloned.1.call-update) | async-done | bytes 2949136 | tf_op jit(solution)/shard_map/all_gather | solution.py:210
  171.6 14.7 %all_to_all.40 = bf16[4,256,384]{2,1,0:T(8,128)(2,1)} all-to-all(bf16[4,256,384]{2,1,0:T(8,128)(2,1)S(1)} %bitcast.93), channel_id=1, replica_groups=mesh['seq'=4,'fsdp'=4,'replica'=2] {'seq'}, dimensions={0} | all-to-all | bytes 1572864 | tf_op jit(solution)/shard_map/all_to_all | solution.py:236
  194.2 7.4 %all-to-all-done.3 = bf16[4,256,384]{2,1,0:T(8,128)(2,1)S(1)} async-done(((bf16[4,256,384]{2,1,0:T(8,128)(2,1)}), bf16[4,256,384]{2,1,0:T(8,128)(2,1)S(1)}, u32[]{:S(2)}, u32[]{:S(2)}) %all-to-all-start.3) | async-done | bytes 786464 | tf_op jit(solution)/shard_map/all_to_all | solution.py:236
  212.7 8.4 %fusion.29 = f32[4,256,3072]{2,1,0:T(8,128)} fusion(bf16[768,1920]{1,0:T(8,128)(2,1)S(1)} %get-tuple-element.95, bf16[768,1920]{1,0:T(8,128)(2,1)S(1)} %get-tuple-element.96, f32[4,256,768]{2,1,0:T(8,128)S(1)} %get-tuple-element.143, f32[768]{0:T(1024)S(1)} %get-tuple-element.78, f32[768]{0:T(1024)S(1)} %get-tuple-element.76, f32[4,256]{1,0:T(4,128)S(1)} %fusion.43, ...), kind=kOutput, calls=%fused_computation.63 | convolution fusion | flops 4845207552 | bytes 21641216 | tf_op jit(solution)/shard_map/tyr,rw->tyw/dot_general | solution.py:374
  221.1 10.9 %bitcast_convert_fusion = bf16[3072,768]{1,0:T(8,128)(2,1)S(1)} fusion(bf16[4,256,768]{2,1,0:T(8,128)(2,1)S(1)} %copy-done.21, f32[4,256,3072]{2,1,0:T(8,128)} %fusion.29, f32[3072]{0:T(1024)S(1)} %add.293), kind=kOutput, calls=%fused_computation.14 | convolution fusion | flops 4865654784 | bytes 18886656 | tf_op jit(solution)/shard_map/ezg,ezv->gv/dot_general | solution.py:395
  232.0 19.5 %fusion.67 = (f32[3072]{0:T(1024)}, bf16[4,256,3072]{2,1,0:T(8,128)(2,1)}) fusion(f32[4,256,3072]{2,1,0:T(8,128)} %fusion.29, f32[3072]{0:T(1024)S(1)} %add.293, bf16[4,256,768]{2,1,0:T(8,128)(2,1)S(1)} %copy-done.21, bf16[3072,384]{1,0:T(8,128)(2,1)} %get-tuple-element.99, bf16[3072,384]{1,0:T(8,128)(2,1)S(1)} %get-tuple-element.98), kind=kOutput, calls=%fused_computation.199 | convolution fusion | flops 4910478336 | bytes 25190400 | tf_op jit(solution)/shard_map/tuy,qy->tuq/dot_general | solution.py:398
  251.5 9.9 %multiply_reduce_fusion = (f32[768]{0:T(1024)}, f32[4,256]{1,0:T(4,128)S(1)}, f32[768]{0:T(1024)}, f32[4,256,768]{2,1,0:T(8,128)S(1)}) fusion(f32[4,256,768]{2,1,0:T(8,128)S(1)} %get-tuple-element.143, f32[4,256]{1,0:T(4,128)S(1)} %fusion.43, f32[4,256]{1,0:T(4,128)S(1)} %broadcast_multiply_fusion, f32[768]{0:T(1024)S(1)} %get-tuple-element.76, ...), kind=kOutput, calls=%fused_computation.49 | convolution fusion | flops 4847563776 | bytes 18502656 | tf_op jit(solution)/shard_map/naz,ez->nae/dot_general | solution.py:409
  261.4 10.4 %bitcast_convert_fusion.1 = bf16[768,3072]{1,0:T(8,128)(2,1)} fusion(bf16[4,256,3072]{2,1,0:T(8,128)(2,1)} %get-tuple-element.147, f32[4,256,768]{2,1,0:T(8,128)S(1)} %get-tuple-element.143, f32[768]{0:T(1024)S(1)} %get-tuple-element.78, f32[768]{0:T(1024)S(1)} %get-tuple-element.76, f32[4,256]{1,0:T(4,128)S(1)} %fusion.43, ...), kind=kOutput, calls=%fused_computation.15 | convolution fusion | flops 4838129664 | bytes 14170112 | tf_op jit(solution)/shard_map/zng,znw->gw/dot_general | solution.py:403
  274.7 4.5 convolution_convert_fusion
  289.6 4.4 add_convert_fusion.1
  293.9 7.2 %all-to-all-done.5 = bf16[4,256,384]{2,1,0:T(8,128)(2,1)S(1)} async-done(((bf16[4,256,384]{2,1,0:T(8,128)(2,1)}), bf16[4,256,384]{2,1,0:T(8,128)(2,1)S(1)}, u32[]{:S(2)}, u32[]{:S(2)}) %all-to-all-start.5) | async-done | bytes 786464 | tf_op jit(solution)/shard_map/all_to_all | solution.py:226
  301.2 4.4 all-to-all-start.4
  305.6 4.4 add_convert_fusion.2
  310.0 7.3 %all-to-all-done.4 = bf16[4,256,384]{2,1,0:T(8,128)(2,1)} async-done(((bf16[4,256,384]{2,1,0:T(8,128)(2,1)}), bf16[4,256,384]{2,1,0:T(8,128)(2,1)}, u32[]{:S(2)}, u32[]{:S(2)}) %all-to-all-start.4) | async-done | bytes 786464 | tf_op jit(solution)/shard_map/all_to_all | solution.py:226
  322.1 19.8 %shard_map.205 = (bf16[1,1024,384]{2,1,0:T(8,128)(2,1)S(1)}, bf16[1,1024,384]{2,1,0:T(8,128)(2,1)S(1)}, bf16[1,1024,384]{2,1,0:T(8,128)(2,1)S(1)}) custom-call(bf16[1,1024,1152]{2,1,0:T(8,128)(2,1)S(1)} %bitcast.89, bf16[1,1024,1152]{2,1,0:T(8,128)(2,1)S(1)} %bitcast.90, bf16[1,1024,1152]{2,1,0:T(8,128)(2,1)S(1)} %bitcast.91, ...), custom_call_target="tpu_custom_call" | custom-call | flops 16106127360 | bytes 5505024 | tf_op jit(solution)/shard_map/pallas_call | solution.py:183
  350.2 4.7 all-to-all-start.6
  360.9 19.2 %shard_map.206 = (bf16[1,1024,384]{2,1,0:T(8,128)(2,1)S(1)}, bf16[1,1024,384]{2,1,0:T(8,128)(2,1)S(1)}, bf16[1,1024,384]{2,1,0:T(8,128)(2,1)S(1)}) custom-call(bf16[1,1024,1152]{2,1,0:T(8,128)(2,1)S(1)} %bitcast.83, bf16[1,1024,1152]{2,1,0:T(8,128)(2,1)S(1)} %bitcast.84, bf16[1,1024,1152]{2,1,0:T(8,128)(2,1)S(1)} %bitcast.85, ...), custom_call_target="tpu_custom_call" | custom-call | flops 16106127360 | bytes 5505024 | tf_op jit(solution)/shard_map/pallas_call | solution.py:183
  381.9 14.1 %collective-permute-done.8 = bf16[4,96,768]{2,1,0:T(8,128)(2,1)S(1)} collective-permute-done((bf16[4,96,768]{2,1,0:T(8,128)(2,1)S(1)}, bf16[4,96,768]{2,1,0:T(8,128)(2,1)S(1)}, u32[]{:S(2)}, u32[]{:S(2)}) %collective-permute-start.8) | collective-permute-done | bytes 589856 | tf_op jit(solution)/shard_map/ppermute | solution.py:201
  411.3 17.1 %all-to-all-done.7 = bf16[4,256,1152]{2,1,0:T(8,128)(2,1)S(1)} async-done(((bf16[4,256,1152]{2,1,0:T(8,128)(2,1)}), bf16[4,256,1152]{2,1,0:T(8,128)(2,1)S(1)}, u32[]{:S(2)}, u32[]{:S(2)}) %all-to-all-start.7) | async-done | bytes 2359328 | tf_op jit(solution)/shard_map/all_to_all | solution.py:236
  439.3 6.6 %fusion.52 = (f32[768]{0:T(1024)S(1)}, f32[4,256]{1,0:T(4,128)S(1)}, f32[4,256,768]{2,1,0:T(8,128)S(1)}) fusion(f32[768]{0:T(1024)S(1)} %copy-done.48, f32[4,256]{1,0:T(4,128)S(1)} %copy-done.45, bf16[4,256,768]{2,1,0:T(8,128)(2,1)S(1)} %copy-done.11, bf16[4,256,2304]{2,1,0:T(8,128)(2,1)} %slice_dynamic-update-slice_fusion, ...), kind=kOutput, calls=%fused_computation.189 | convolution fusion | flops 3635673344 | bytes 12990464 | tf_op jit(solution)/shard_map/wri,yi->wry/dot_general | solution.py:481
  452.0 6.8 %bitcast_convert_fusion.2 = bf16[768,2304]{1,0:T(8,128)(2,1)S(1)} fusion(bf16[4,256,2304]{2,1,0:T(8,128)(2,1)} %slice_dynamic-update-slice_fusion, bf16[4,256,768]{2,1,0:T(8,128)(2,1)S(1)} %copy-done.11, f32[768]{0:T(1024)S(1)} %copy-done.61, f32[768]{0:T(1024)S(1)} %copy-done.48, f32[4,256]{1,0:T(4,128)S(1)} %copy-done.50, f32[4,256]{1,0:T(4,128)S(1)} %copy-done.45), kind=kOutput, calls=%fused_computation.18 | convolution fusion | flops 3630366720 | bytes 9844736 | tf_op jit(solution)/shard_map/azk,azx->kx/dot_general | solution.py:478
  472.6 11.9 %add_convert_fusion.3 = bf16[4,256,768]{2,1,0:T(8,128)(2,1)} fusion(f32[4,256,768]{2,1,0:T(8,128)S(1)} %copy-done.13, f32[768]{0:T(1024)S(1)} %copy-done.59, bf16[3072,384]{1,0:T(8,128)(2,1)S(1)} %copy-done.33, bf16[3072,384]{1,0:T(8,128)(2,1)S(1)} %copy-done.32, f32[4,256,3072]{2,1,0:T(8,128)} %fusion.29, f32[3072]{0:T(1024)S(1)} %copy-done.58), kind=kOutput, calls=%fused_computation.55 | convolution fusion | flops 4875091968 | bytes 22035456 | tf_op jit(solution)/shard_map/crx,xo->cro/dot_general | solution.py:385
  495.8 8.8 %collective-permute-done.10 = bf16[4,192,384]{2,1,0:T(8,128)(2,1)S(1)} collective-permute-done((bf16[4,192,384]{2,1,0:T(8,128)(2,1)S(1)}, bf16[4,192,384]{2,1,0:T(8,128)(2,1)S(1)}, u32[]{:S(2)}, u32[]{:S(2)}) %collective-permute-start.10) | collective-permute-done | bytes 589856 | tf_op jit(solution)/shard_map/ppermute | solution.py:201
  510.7 6.3 %collective-permute-done.11 = bf16[4,192,192]{2,1,0:T(8,128)(2,1)S(1)} collective-permute-done((bf16[4,192,192]{2,1,0:T(8,128)(2,1)S(1)}, bf16[4,192,192]{2,1,0:T(8,128)(2,1)S(1)}, u32[]{:S(2)}, u32[]{:S(2)}) %collective-permute-start.11) | collective-permute-done | bytes 294944 | tf_op jit(solution)/shard_map/ppermute | solution.py:201
  527.3 12.5 %reduce-scatter.3.cloned.1.call-done = bf16[1,192,384]{2,1,0:T(8,128)(2,1)} async-done(((bf16[4,192,384]{2,1,0:T(8,128)(2,1)}), bf16[1,192,384]{2,1,0:T(8,128)(2,1)}) %reduce-scatter.3.cloned.1.call-update) | async-done | bytes 147472 | tf_op jit(solution)/shard_map/reduce_scatter | solution.py:279
  549.0 6.0 %multiply_subtract_fusion.1 = (f32[768,768]{1,0:T(8,128)}, f32[768,768]{1,0:T(8,128)}, f32[768,768]{1,0:T(8,128)}) fusion(f32[768,768]{1,0:T(8,128)S(1)} %copy-done.19, bf16[384,768]{1,0:T(8,128)(2,1)S(1)} %get-tuple-element.113, bf16[384,768]{1,0:T(8,128)(2,1)S(1)} %get-tuple-element.112, f32[768,768]{1,0:T(8,128)S(1)} %copy-done.34, f32[768,768]{1,0:T(8,128)} %param.20), kind=kLoop, calls=%fused_computation.72 | loop fusion | flops 11206656 | bytes 15335424 | tf_op jit(solution)/shard_map/sub | solution.py:40
  563.7 8.7 %multiply_subtract_fusion = (f32[192,6144]{1,0:T(8,128)}, f32[192,6144]{1,0:T(8,128)}, f32[192,6144]{1,0:T(8,128)}) fusion(f32[192,6144]{1,0:T(8,128)S(1)} %bitcast.95, bf16[192,6144]{1,0:T(8,128)(2,1)S(1)} %select_dynamic-update-slice_fusion, f32[192,6144]{1,0:T(8,128)} %param.16, f32[192,6144]{1,0:T(8,128)} %param.17), kind=kLoop, calls=%fused_computation.35 | loop fusion | flops 18874368 | bytes 30670848 | tf_op jit(solution)/shard_map/sub | solution.py:40
  (333 shorter events, 187.5 us)
Async XLA Ops:
  7.2 51.1 %all-gather.4.cloned.1.call-start = ((), (), s32[]{:S(2)}) async-start(), calls=%async_computation.10 | async-start | bytes 2457600 | tf_op jit(solution)/shard_map/all_gather | solution.py:318
  11.9 145.9 %all-gather.8.cloned.1.call-start = ((), (), s32[]{:S(2)}) async-start(), calls=%async_computation.12 | async-start | bytes 2949120 | tf_op jit(solution)/shard_map/all_gather | solution.py:210
  59.2 111.8 %all-gather.6.cloned.1.call-start = ((), (), s32[]{:S(2)}) async-start(), calls=%async_computation.11 | async-start | bytes 3686400 | tf_op jit(solution)/shard_map/all_gather | solution.py:210
  77.3 32.1 %all-to-all-start = ((bf16[4,256,1152]{2,1,0:T(8,128)(2,1)}), bf16[4,256,1152]{2,1,0:T(8,128)(2,1)S(1)}, u32[]{:S(2)}, u32[]{:S(2)}) async-start(bf16[4,256,1152]{2,1,0:T(8,128)(2,1)} %pad_maximum_fusion.2), calls=%async_computation | async-start | bytes 4718592 | tf_op jit(solution)/shard_map/all_to_all | solution.py:226
  110.8 32.3 %all-to-all-start.1 = ((bf16[4,256,1152]{2,1,0:T(8,128)(2,1)}), bf16[4,256,1152]{2,1,0:T(8,128)(2,1)S(1)}, u32[]{:S(2)}, u32[]{:S(2)}) async-start(bf16[4,256,1152]{2,1,0:T(8,128)(2,1)} %pad_maximum_fusion.3), calls=%async_computation.1 | async-start | bytes 4718592 | tf_op jit(solution)/shard_map/all_to_all | solution.py:226
  171.0 31.5 %collective-permute-start.2 = (bf16[3072,384]{1,0:T(8,128)(2,1)}, bf16[3072,384]{1,0:T(8,128)(2,1)}, u32[]{:S(2)}, u32[]{:S(2)}) collective-permute-start(bf16[3072,384]{1,0:T(8,128)(2,1)} %all-gather.8.cloned.1.call-done), channel_id=1, source_target_pairs={{0,8},{8,0},{16,24},{24,16},{1,9},{9,1},{17,25},{25,17},{2,10},{10... | collective-permute-start | bytes 7077896 | tf_op jit(solution)/shard_map/ppermute | solution.py:201
  171.0 35.9 %collective-permute-start.1 = (bf16[768,1920]{1,0:T(8,128)(2,1)}, bf16[768,1920]{1,0:T(8,128)(2,1)}, u32[]{:S(2)}, u32[]{:S(2)}) collective-permute-start(bf16[768,1920]{1,0:T(8,128)(2,1)} %all-gather.6.cloned.1.call-done), channel_id=1, source_target_pairs={{0,8},{8,0},{16,24},{24,16},{1,9},{9,1},{17,25},{25,17},{2,10},{10... | collective-permute-start | bytes 8847368 | tf_op jit(solution)/shard_map/ppermute | solution.py:201
  186.3 15.3 %all-to-all-start.3 = ((bf16[4,256,384]{2,1,0:T(8,128)(2,1)}), bf16[4,256,384]{2,1,0:T(8,128)(2,1)S(1)}, u32[]{:S(2)}, u32[]{:S(2)}) async-start(bf16[4,256,384]{2,1,0:T(8,128)(2,1)} %bitcast.8), calls=%async_computation.3 | async-start | bytes 1572864 | tf_op jit(solution)/shard_map/all_to_all | solution.py:236
  280.8 8.8 %collective-permute-start.4 = (bf16[4,384,768]{2,1,0:T(8,128)(2,1)}, bf16[4,384,768]{2,1,0:T(8,128)(2,1)}, u32[]{:S(2)}, u32[]{:S(2)}) collective-permute-start(bf16[4,384,768]{2,1,0:T(8,128)(2,1)} %constant_dynamic-slice_fusion.10), channel_id=1, source_target_pairs={{0,8},{8,0},{16,24},{24,16},{1,9},{9,1},{17,25},{25,17},{2,10},{10... | collective-permute-start | bytes 7077896 | tf_op jit(solution)/shard_map/ppermute | solution.py:201
  284.1 21.4 %collective-permute-start.3 = (bf16[4,192,1536]{2,1,0:T(8,128)(2,1)}, bf16[4,192,1536]{2,1,0:T(8,128)(2,1)}, u32[]{:S(2)}, u32[]{:S(2)}) collective-permute-start(bf16[4,192,1536]{2,1,0:T(8,128)(2,1)} %constant_dynamic-slice_fusion.11), channel_id=1, source_target_pairs={{0,8},{8,0},{16,24},{24,16},{1,9},{9,1},{17,25},{25,17},{2,10},{10... | collective-permute-start | bytes 7077896 | tf_op jit(solution)/shard_map/ppermute | solution.py:201
  286.0 15.1 %all-to-all-start.5 = ((bf16[4,256,384]{2,1,0:T(8,128)(2,1)}), bf16[4,256,384]{2,1,0:T(8,128)(2,1)S(1)}, u32[]{:S(2)}, u32[]{:S(2)}) async-start(bf16[4,256,384]{2,1,0:T(8,128)(2,1)} %get-tuple-element.110), calls=%async_computation.5 | async-start | bytes 1572864 | tf_op jit(solution)/shard_map/all_to_all | solution.py:226
  301.2 16.1 %all-to-all-start.4 = ((bf16[4,256,384]{2,1,0:T(8,128)(2,1)}), bf16[4,256,384]{2,1,0:T(8,128)(2,1)}, u32[]{:S(2)}, u32[]{:S(2)}) async-start(bf16[4,256,384]{2,1,0:T(8,128)(2,1)} %get-tuple-element.111), calls=%async_computation.4 | async-start | bytes 1572864 | tf_op jit(solution)/shard_map/all_to_all | solution.py:226
  318.7 27.6 %collective-permute-start.6 = (bf16[4,192,768]{2,1,0:T(8,128)(2,1)S(1)}, bf16[4,192,768]{2,1,0:T(8,128)(2,1)S(1)}, u32[]{:S(2)}, u32[]{:S(2)}) collective-permute-start(bf16[4,192,768]{2,1,0:T(8,128)(2,1)S(1)} %constant_dynamic-slice_fusion.8), channel_id=1, source_target_pairs={{0,1},{1,0},{2,3},{3,2},{4,5},{5,4},{6,7},{7,6},{8,9},{9,8},{10,11... | collective-permute-start | bytes 3538952 | tf_op jit(solution)/shard_map/ppermute | solution.py:201
  321.6 27.3 %collective-permute-start.5 = (bf16[4,192,768]{2,1,0:T(8,128)(2,1)S(1)}, bf16[4,192,768]{2,1,0:T(8,128)(2,1)S(1)}, u32[]{:S(2)}, u32[]{:S(2)}) collective-permute-start(bf16[4,192,768]{2,1,0:T(8,128)(2,1)S(1)} %constant_dynamic-slice_fusion.9), channel_id=1, source_target_pairs={{0,16},{8,24},{16,0},{24,8},{1,17},{9,25},{17,1},{25,9},{2,18},{10... | collective-permute-start | bytes 3538952 | tf_op jit(solution)/shard_map/ppermute | solution.py:201
  350.2 46.0 %all-to-all-start.6 = ((bf16[4,256,1152]{2,1,0:T(8,128)(2,1)}), bf16[4,256,1152]{2,1,0:T(8,128)(2,1)}, u32[]{:S(2)}, u32[]{:S(2)}) async-start(bf16[4,256,1152]{2,1,0:T(8,128)(2,1)} %bitcast.97), calls=%async_computation.6 | async-start | bytes 4718592 | tf_op jit(solution)/shard_map/all_to_all | solution.py:236
  356.1 25.7 %collective-permute-start.7 = (bf16[4,192,384]{2,1,0:T(8,128)(2,1)S(1)}, bf16[4,192,384]{2,1,0:T(8,128)(2,1)S(1)}, u32[]{:S(2)}, u32[]{:S(2)}) collective-permute-start(bf16[4,192,384]{2,1,0:T(8,128)(2,1)S(1)} %constant_dynamic-slice_fusion.7), channel_id=1, source_target_pairs={{0,1},{1,0},{2,3},{3,2},{4,5},{5,4},{6,7},{7,6},{8,9},{9,8},{10,11... | collective-permute-start | bytes 1769480 | tf_op jit(solution)/shard_map/ppermute | solution.py:201
  357.8 38.2 %collective-permute-start.8 = (bf16[4,96,768]{2,1,0:T(8,128)(2,1)S(1)}, bf16[4,96,768]{2,1,0:T(8,128)(2,1)S(1)}, u32[]{:S(2)}, u32[]{:S(2)}) collective-permute-start(bf16[4,96,768]{2,1,0:T(8,128)(2,1)S(1)} %constant_dynamic-slice_fusion.6), channel_id=1, source_target_pairs={{0,16},{8,24},{16,0},{24,8},{1,17},{9,25},{17,1},{25,9},{2,18},{10... | collective-permute-start | bytes 1769480 | tf_op jit(solution)/shard_map/ppermute | solution.py:201
  396.2 32.1 %all-to-all-start.7 = ((bf16[4,256,1152]{2,1,0:T(8,128)(2,1)}), bf16[4,256,1152]{2,1,0:T(8,128)(2,1)S(1)}, u32[]{:S(2)}, u32[]{:S(2)}) async-start(bf16[4,256,1152]{2,1,0:T(8,128)(2,1)} %bitcast.96), calls=%async_computation.7 | async-start | bytes 4718592 | tf_op jit(solution)/shard_map/all_to_all | solution.py:236
  399.8 85.5 %reduce-scatter.5.cloned.1.call-start = ((), (), s32[]{:S(2)}) async-start(), calls=%async_computation.14 | async-start | bytes 1474560 | tf_op jit(solution)/shard_map/reduce_scatter | solution.py:279
  408.7 131.2 %reduce-scatter.3.cloned.1.call-start = ((), (), s32[]{:S(2)}) async-start(), calls=%async_computation.13 | async-start | bytes 737280 | tf_op jit(solution)/shard_map/reduce_scatter | solution.py:279
  468.4 20.4 %collective-permute-start.9 = (bf16[4,192,768]{2,1,0:T(8,128)(2,1)}, bf16[4,192,768]{2,1,0:T(8,128)(2,1)}, u32[]{:S(2)}, u32[]{:S(2)}) collective-permute-start(bf16[4,192,768]{2,1,0:T(8,128)(2,1)} %constant_dynamic-slice_fusion.5), channel_id=1, source_target_pairs={{0,8},{8,0},{16,24},{24,16},{1,9},{9,1},{17,25},{25,17},{2,10},{10... | collective-permute-start | bytes 3538952 | tf_op jit(solution)/shard_map/ppermute | solution.py:201
  468.4 24.1 %collective-permute-start.12 = (bf16[4,192,768]{2,1,0:T(8,128)(2,1)S(1)}, bf16[4,192,768]{2,1,0:T(8,128)(2,1)}, u32[]{:S(2)}, u32[]{:S(2)}) collective-permute-start(bf16[4,192,768]{2,1,0:T(8,128)(2,1)S(1)} %constant_dynamic-slice_fusion.2), channel_id=1, source_target_pairs={{0,8},{8,0},{16,24},{24,16},{1,9},{9,1},{17,25},{25,17},{2,10},{10... | collective-permute-start | bytes 3538952 | tf_op jit(solution)/shard_map/ppermute | solution.py:201
  471.4 13.2 %collective-permute-start.31 = (f32[12,768]{1,0:T(8,128)S(1)}, f32[12,768]{1,0:T(8,128)S(1)}, u32[]{:S(2)}, u32[]{:S(2)}) collective-permute-start(f32[12,768]{1,0:T(8,128)S(1)} %add.346), channel_id=1, source_target_pairs={{0,4},{2,6},{4,0},{6,2},{1,5},{3,7},{5,1},{7,3},{8,12},{10,14},{12... | collective-permute-start | bytes 110600 | tf_op jit(solution)/shard_map/ppermute | solution.py:201
  488.3 30.3 %collective-permute-start.21 = (bf16[192,384]{1,0:T(8,128)(2,1)}, bf16[192,384]{1,0:T(8,128)(2,1)}, u32[]{:S(2)}, u32[]{:S(2)}) collective-permute-start(bf16[192,384]{1,0:T(8,128)(2,1)} %slice.170), channel_id=1, source_target_pairs={{0,1},{1,0},{2,3},{3,2},{4,5},{5,4},{6,7},{7,6},{8,9},{9,8},{10,11... | collective-permute-start | bytes 442376 | tf_op jit(solution)/shard_map/ppermute | solution.py:201
  490.8 13.8 %collective-permute-start.10 = (bf16[4,192,384]{2,1,0:T(8,128)(2,1)S(1)}, bf16[4,192,384]{2,1,0:T(8,128)(2,1)S(1)}, u32[]{:S(2)}, u32[]{:S(2)}) collective-permute-start(bf16[4,192,384]{2,1,0:T(8,128)(2,1)S(1)} %constant_dynamic-slice_fusion.4), channel_id=1, source_target_pairs={{0,16},{8,24},{16,0},{24,8},{1,17},{9,25},{17,1},{25,9},{2,18},{10... | collective-permute-start | bytes 1769480 | tf_op jit(solution)/shard_map/ppermute | solution.py:201
  494.2 13.0 %collective-permute-start.13 = (bf16[4,192,384]{2,1,0:T(8,128)(2,1)S(1)}, bf16[4,192,384]{2,1,0:T(8,128)(2,1)S(1)}, u32[]{:S(2)}, u32[]{:S(2)}) collective-permute-start(bf16[4,192,384]{2,1,0:T(8,128)(2,1)S(1)} %constant_dynamic-slice_fusion.1), channel_id=1, source_target_pairs={{0,1},{1,0},{2,3},{3,2},{4,5},{5,4},{6,7},{7,6},{8,9},{9,8},{10,11... | collective-permute-start | bytes 1769480 | tf_op jit(solution)/shard_map/ppermute | solution.py:201
  505.0 12.1 %collective-permute-start.11 = (bf16[4,192,192]{2,1,0:T(8,128)(2,1)S(1)}, bf16[4,192,192]{2,1,0:T(8,128)(2,1)S(1)}, u32[]{:S(2)}, u32[]{:S(2)}) collective-permute-start(bf16[4,192,192]{2,1,0:T(8,128)(2,1)S(1)} %constant_dynamic-slice_fusion.3), channel_id=1, source_target_pairs={{0,1},{1,0},{2,3},{3,2},{4,5},{5,4},{6,7},{7,6},{8,9},{9,8},{10,11... | collective-permute-start | bytes 884744 | tf_op jit(solution)/shard_map/ppermute | solution.py:201
  507.6 9.7 %collective-permute-start.14 = (bf16[4,192,192]{2,1,0:T(8,128)(2,1)S(1)}, bf16[4,192,192]{2,1,0:T(8,128)(2,1)S(1)}, u32[]{:S(2)}, u32[]{:S(2)}) collective-permute-start(bf16[4,192,192]{2,1,0:T(8,128)(2,1)S(1)} %constant_dynamic-slice_fusion), channel_id=1, source_target_pairs={{0,16},{8,24},{16,0},{24,8},{1,17},{9,25},{17,1},{25,9},{2,18},{10... | collective-permute-start | bytes 884744 | tf_op jit(solution)/shard_map/ppermute | solution.py:201
  509.9 11.2 %collective-permute-start.25 = (bf16[192,768]{1,0:T(8,128)(2,1)S(1)}, bf16[192,768]{1,0:T(8,128)(2,1)S(1)}, u32[]{:S(2)}, u32[]{:S(2)}) collective-permute-start(bf16[192,768]{1,0:T(8,128)(2,1)S(1)} %pad_maximum_fusion.13), channel_id=1, source_target_pairs={{0,1},{1,0},{2,3},{3,2},{4,5},{5,4},{6,7},{7,6},{8,9},{9,8},{10,11... | collective-permute-start | bytes 884744 | tf_op jit(solution)/shard_map/ppermute | solution.py:201
  522.2 22.1 %collective-permute-start.26 = (bf16[384,768]{1,0:T(8,128)(2,1)}, bf16[384,768]{1,0:T(8,128)(2,1)}, u32[]{:S(2)}, u32[]{:S(2)}) collective-permute-start(bf16[384,768]{1,0:T(8,128)(2,1)} %pad_maximum_fusion.9), channel_id=1, source_target_pairs={{0,8},{8,0},{16,24},{24,16},{1,9},{9,1},{17,25},{25,17},{2,10},{10... | collective-permute-start | bytes 1769480 | tf_op jit(solution)/shard_map/ppermute | solution.py:201
  527.3 34.9 %collective-permute-start.23 = (bf16[192,1536]{1,0:T(8,128)(2,1)}, bf16[192,1536]{1,0:T(8,128)(2,1)}, u32[]{:S(2)}, u32[]{:S(2)}) collective-permute-start(bf16[192,1536]{1,0:T(8,128)(2,1)} %pad_maximum_fusion.8), channel_id=1, source_target_pairs={{0,8},{8,0},{16,24},{24,16},{1,9},{9,1},{17,25},{25,17},{2,10},{10... | collective-permute-start | bytes 1769480 | tf_op jit(solution)/shard_map/ppermute | solution.py:201
  548.4 8.4 %collective-permute-start.16 = (bf16[192,384]{1,0:T(8,128)(2,1)S(1)}, bf16[192,384]{1,0:T(8,128)(2,1)S(1)}, u32[]{:S(2)}, u32[]{:S(2)}) collective-permute-start(bf16[192,384]{1,0:T(8,128)(2,1)S(1)} %pad_maximum_fusion.14), channel_id=1, source_target_pairs={{0,16},{8,24},{16,0},{24,8},{1,17},{9,25},{17,1},{25,9},{2,18},{10... | collective-permute-start | bytes 442376 | tf_op jit(solution)/shard_map/ppermute | solution.py:201
  (77 other events, 722.2 us)
Sparse Core Ops, SparseCore 0:
  12.0 46.2 all-gather.3
  60.4 49.3 all-gather.7
  111.9 59.0 all-gather.5
  408.8 27.4 reduce-scatter.4
  518.7 21.1 reduce-scatter.2
